TPU v7x, 32 devices: a whole 2x2x4 slice. The times are simulated.
32 devices in a mesh: clip: 4 (over z), seq: 2 (over x), fsdp: 4 (over y, core).
Axes of the slice: x: 2, y: 2, z: 4, core: 2. Of those that a mesh axis runs over, the one named last changes fastest.
Arguments:
- tokens: bfloat16 [2, 16, 16, 128, 768], P(None, ('clip', 'fsdp'), 'seq'), may hold values from -6 to 6
- cotangent: bfloat16 [2, 16, 16, 128, 768], P(None, ('clip', 'fsdp'), 'seq'), may hold values from -6 to 6
- weights: float32 [16, 768, 768], P(('clip', 'fsdp'), 'seq'), may hold values from -0.8660254 to 0.8660254, as said below
- momentum: float32 [16, 768, 768], P(('clip', 'fsdp'), 'seq'), may hold values from -448 to 448
- vectors: float32 [17, 768], replicated, may hold values from -1.2 to 1.4
Outputs:
- mixed: bfloat16 [2, 16, 16, 128, 768], P(None, ('clip', 'fsdp'), 'seq')
- input_grad: bfloat16 [2, 16, 16, 128, 768], P(None, ('clip', 'fsdp'), 'seq')
- new_momentum: float32 [16, 768, 768], P(('clip', 'fsdp'), 'seq')
- new_weights: float32 [16, 768, 768], P(('clip', 'fsdp'), 'seq')
- new_low: bfloat16 [16, 768, 768], P(('clip', 'fsdp'), 'seq')
- vector_grads: float32 [17, 768], replicated
- new_vectors: float32 [17, 768], replicated
Inputs may be any that keep to these rules, and one draw needn't show every extreme that they name: `weights`: weight blocks scaled by their fan-in.
All inputs are finite; a program needn't handle non-finite values.
Results may differ from a plain program's by a relative error of at most 0.018.
Values may be sent and summed in bfloat16 or wider, within the bound.
A program may use at most 448 MiB of HBM per device.

v0:
```python
import jax
import jax.numpy as jnp
from jax import lax
from jax.sharding import PartitionSpec as P

HEADS = 12
HEAD = 64
FRAMES = 16
PATCHES = 128
NS_STEPS = 2


EPS_NORM = 1e-06
NS_A = 3.4445
NS_B = -4.775
NS_C = 2.0315
DECAY = 0.5
MUON_RATE = 0.5
VECTOR_RATE = 0.2
HIGHEST = lax.Precision.HIGHEST


def factor_of(matrix_index):
    return (
        1.0
        + 3.0 * (matrix_index == 3).astype(jnp.float32)
        + (matrix_index == 7).astype(jnp.float32)
        - 0.5 * (matrix_index >= 12).astype(jnp.float32)
    )


def pattern(left_form, right_form, result_form):
    return left_form + "," + right_form + "->" + result_form


def heads_view(values):
    return values.reshape(values.shape[:-1] + (HEADS, HEAD))


def flat_view(values):
    return values.reshape(values.shape[:-2] + (HEADS * HEAD,))


def multiply(values, matrix):
    return jnp.einsum("...d,de->...e", values, matrix, preferred_element_type=jnp.float32)


def multiply_back(grads, matrix):
    return jnp.einsum("...e,de->...d", grads, matrix, preferred_element_type=jnp.float32)


def outer_sum(values, grads):
    return jnp.einsum("...d,...e->de", values, grads, preferred_element_type=jnp.float32)


def token_sum(values):
    return jnp.sum(values.reshape((-1,) + values.shape[-1:]).astype(jnp.float32), 0)


def exact_gelu(values):
    return jax.nn.gelu(values, approximate=False)


def norm_forward(values, gain_row, offset):
    average = jnp.mean(values, -1, keepdims=True)
    centred = values - average
    inverse = lax.rsqrt(jnp.mean(centred * centred, -1, keepdims=True) + EPS_NORM)
    normal = centred * inverse
    return (normal, inverse, normal * gain_row + offset)


def norm_backward(grads, normal, inverse, gain_row):
    scaled = grads * gain_row
    back = inverse * (
        scaled
        - jnp.mean(scaled, -1, keepdims=True)
        - normal * jnp.mean(scaled * normal, -1, keepdims=True)
    )
    return (back, token_sum(grads * normal), token_sum(grads))


def scores_of(queries, key_heads, forms, score_scale):
    return (
        jnp.einsum(
            pattern(forms[0], forms[1], forms[2]),
            queries,
            key_heads,
            preferred_element_type=jnp.float32,
        )
        * score_scale
    )


def attention_core(queries, key_heads, value_heads, forms, score_scale):
    scores = scores_of(queries, key_heads, forms, score_scale)
    log_total = jax.nn.logsumexp(scores, axis=-1, keepdims=True)
    chances = jnp.exp(scores - log_total).astype(jnp.bfloat16)
    attended = jnp.einsum(
        pattern(forms[2], forms[1], forms[0]),
        chances,
        value_heads,
        preferred_element_type=jnp.float32,
    )
    return (attended, log_total)


def attention_grads(queries, key_heads, value_heads, log_total, grad_attended, forms, score_scale):
    chances = jnp.exp(scores_of(queries, key_heads, forms, score_scale) - log_total)
    chances_low = chances.astype(jnp.bfloat16)
    grad_chances = jnp.einsum(
        pattern(forms[0], forms[1], forms[2]),
        grad_attended,
        value_heads,
        preferred_element_type=jnp.float32,
    )
    grad_value = jnp.einsum(
        pattern(forms[2], forms[0], forms[1]),
        chances_low,
        grad_attended,
        preferred_element_type=jnp.float32,
    )
    grad_scores = (
        chances * (grad_chances - jnp.sum(grad_chances * chances, -1, keepdims=True))
    ).astype(jnp.bfloat16)
    grad_query = (
        jnp.einsum(
            pattern(forms[2], forms[1], forms[0]),
            grad_scores,
            key_heads,
            preferred_element_type=jnp.float32,
        )
        * score_scale
    )
    grad_key = (
        jnp.einsum(
            pattern(forms[2], forms[0], forms[1]),
            grad_scores,
            queries,
            preferred_element_type=jnp.float32,
        )
        * score_scale
    )
    return (grad_query, grad_key, grad_value)


def project_three(normed_low, weight_stack, first_block, vector_rows, query_row, value_row):
    queries = (multiply(normed_low, weight_stack[first_block]) + vector_rows[query_row]).astype(
        jnp.bfloat16
    )
    key_rows = multiply(normed_low, weight_stack[first_block + 1]).astype(jnp.bfloat16)
    value_rows = (
        multiply(normed_low, weight_stack[first_block + 2]) + vector_rows[value_row]
    ).astype(jnp.bfloat16)
    return (queries, key_rows, value_rows)


def out_back(attended_low, grad_low, w_out):
    d_out = outer_sum(attended_low, grad_low)
    grad_attended = multiply_back(grad_low, w_out).astype(jnp.bfloat16)
    return (d_out, token_sum(grad_low), grad_attended)


def input_back(normed_low, grad_query, grad_key, grad_value, weight_stack, first_block):
    d_query = outer_sum(normed_low, grad_query)
    d_key = outer_sum(normed_low, grad_key)
    d_value = outer_sum(normed_low, grad_value)
    grad_normed = (
        multiply_back(grad_query, weight_stack[first_block])
        + multiply_back(grad_key, weight_stack[first_block + 1])
        + multiply_back(grad_value, weight_stack[first_block + 2])
    )
    return (d_query, d_key, d_value, token_sum(grad_query), token_sum(grad_value), grad_normed)


def layer_pass(tokens_one, cotangent_one, weight_stack, vector_rows):
    score_scale = HEAD ** (-0.5)
    spatial_forms = ("cfqhe", "cfkhe", "cfhqk")
    temporal_forms = ("cqphe", "ckphe", "cphqk")
    start = tokens_one.astype(jnp.float32)
    normal_one, inverse_one, normed = norm_forward(start, vector_rows[0], vector_rows[3])
    normed_one = normed.astype(jnp.bfloat16)
    query_one, key_one, value_one = project_three(normed_one, weight_stack, 0, vector_rows, 6, 7)
    attended, log_one = attention_core(
        heads_view(query_one),
        heads_view(key_one),
        heads_view(value_one),
        spatial_forms,
        score_scale,
    )
    attended_one = flat_view(attended).astype(jnp.bfloat16)
    first = (start + multiply(attended_one, weight_stack[3]) + vector_rows[8]).astype(jnp.bfloat16)
    placed = lax.all_to_all(first, "seq", split_axis=2, concat_axis=1, tiled=True)
    placed_float = placed.astype(jnp.float32)
    normal_two, inverse_two, normed = norm_forward(placed_float, vector_rows[1], vector_rows[4])
    normed_two = normed.astype(jnp.bfloat16)
    query_two, key_two, value_two = project_three(normed_two, weight_stack, 4, vector_rows, 9, 10)
    attended, log_two = attention_core(
        heads_view(query_two),
        heads_view(key_two),
        heads_view(value_two),
        temporal_forms,
        score_scale,
    )
    attended_two = flat_view(attended).astype(jnp.bfloat16)
    second = (placed_float + multiply(attended_two, weight_stack[7]) + vector_rows[11]).astype(
        jnp.bfloat16
    )
    framed = lax.all_to_all(second, "seq", split_axis=1, concat_axis=2, tiled=True)
    framed_float = framed.astype(jnp.float32)
    normal_three, inverse_three, normed = norm_forward(framed_float, vector_rows[2], vector_rows[5])
    normed_three = normed.astype(jnp.bfloat16)
    hidden = (
        jnp.einsum(
            "cfpd,jde->cfpje", normed_three, weight_stack[8:12], preferred_element_type=jnp.float32
        )
        + vector_rows[13:17]
    )
    activated, gelu_pull = jax.vjp(exact_gelu, hidden)
    active_low = activated.astype(jnp.bfloat16)
    output = (
        framed_float
        + jnp.einsum(
            "cfpje,jed->cfpd", active_low, weight_stack[12:16], preferred_element_type=jnp.float32
        )
        + vector_rows[12]
    ).astype(jnp.bfloat16)
    grad_float = cotangent_one.astype(jnp.float32)
    d_down = jnp.einsum(
        "cfpje,cfpd->jed", active_low, cotangent_one, preferred_element_type=jnp.float32
    )
    grad_active = jnp.einsum(
        "cfpd,jed->cfpje", cotangent_one, weight_stack[12:16], preferred_element_type=jnp.float32
    )
    grad_hidden = gelu_pull(grad_active)[0].astype(jnp.bfloat16)
    d_up = jnp.einsum(
        "cfpd,cfpje->jde", normed_three, grad_hidden, preferred_element_type=jnp.float32
    )
    d_bias_up = jnp.sum(grad_hidden.astype(jnp.float32).reshape((-1,) + grad_hidden.shape[-2:]), 0)
    grad_normed = jnp.einsum(
        "cfpje,jde->cfpd", grad_hidden, weight_stack[8:12], preferred_element_type=jnp.float32
    )
    back_three, gain_three, offset_three = norm_backward(
        grad_normed, normal_three, inverse_three, vector_rows[2]
    )
    grad_second = (grad_float + back_three).astype(jnp.bfloat16)
    grad_placed = lax.all_to_all(grad_second, "seq", split_axis=2, concat_axis=1, tiled=True)
    d_out_two, bias_out_two, grad_attended = out_back(attended_two, grad_placed, weight_stack[7])
    grad_query, grad_key, grad_value = attention_grads(
        heads_view(query_two),
        heads_view(key_two),
        heads_view(value_two),
        log_two,
        heads_view(grad_attended),
        temporal_forms,
        score_scale,
    )
    d_query_two, d_key_two, d_value_two, bias_query_two, bias_value_two, grad_normed = input_back(
        normed_two,
        flat_view(grad_query).astype(jnp.bfloat16),
        flat_view(grad_key).astype(jnp.bfloat16),
        flat_view(grad_value).astype(jnp.bfloat16),
        weight_stack,
        4,
    )
    back_two, gain_two, offset_two = norm_backward(
        grad_normed, normal_two, inverse_two, vector_rows[1]
    )
    grad_first = (grad_placed.astype(jnp.float32) + back_two).astype(jnp.bfloat16)
    grad_framed = lax.all_to_all(grad_first, "seq", split_axis=1, concat_axis=2, tiled=True)
    d_out_one, bias_out_one, grad_attended = out_back(attended_one, grad_framed, weight_stack[3])
    grad_query, grad_key, grad_value = attention_grads(
        heads_view(query_one),
        heads_view(key_one),
        heads_view(value_one),
        log_one,
        heads_view(grad_attended),
        spatial_forms,
        score_scale,
    )
    d_query_one, d_key_one, d_value_one, bias_query_one, bias_value_one, grad_normed = input_back(
        normed_one,
        flat_view(grad_query).astype(jnp.bfloat16),
        flat_view(grad_key).astype(jnp.bfloat16),
        flat_view(grad_value).astype(jnp.bfloat16),
        weight_stack,
        0,
    )
    back_one, gain_one, offset_one = norm_backward(
        grad_normed, normal_one, inverse_one, vector_rows[0]
    )
    grad_input = (grad_framed.astype(jnp.float32) + back_one).astype(jnp.bfloat16)
    weight_grads = jnp.concatenate(
        [
            jnp.stack(
                [
                    d_query_one,
                    d_key_one,
                    d_value_one,
                    d_out_one,
                    d_query_two,
                    d_key_two,
                    d_value_two,
                    d_out_two,
                ]
            ),
            d_up,
            d_down,
        ],
        0,
    )
    vector_grads = jnp.concatenate(
        [
            jnp.stack(
                [
                    gain_one,
                    gain_two,
                    gain_three,
                    offset_one,
                    offset_two,
                    offset_three,
                    bias_query_one,
                    bias_value_one,
                    bias_out_one,
                    bias_query_two,
                    bias_value_two,
                    bias_out_two,
                    token_sum(grad_float),
                ]
            ),
            d_bias_up,
        ],
        0,
    )
    return (output, grad_input, weight_grads, vector_grads)


def gather_weights(low_shard):
    row_full = lax.all_gather(low_shard, "seq", axis=1, tiled=True)
    return lax.all_gather(row_full, ("clip", "fsdp"), axis=0, tiled=True)


def reduce_grads(weight_grads):
    owner_part = lax.psum_scatter(
        weight_grads.astype(jnp.bfloat16), ("clip", "fsdp"), scatter_dimension=0, tiled=True
    )
    return lax.psum_scatter(owner_part, "seq", scatter_dimension=1, tiled=True).astype(jnp.float32)


def newton_schulz(matrix):
    current = matrix / (jnp.sqrt(jnp.sum(matrix * matrix)) + 1e-07)
    for sweep_index in range(NS_STEPS):
        gram_matrix = jnp.dot(current, current.T, precision=HIGHEST)
        polynomial = NS_B * gram_matrix + NS_C * jnp.dot(
            gram_matrix, gram_matrix, precision=HIGHEST
        )
        current = NS_A * current + jnp.dot(polynomial, current, precision=HIGHEST)
    return current


def body(tokens, cotangent, weights, momentum, vectors):
    micro_count = tokens.shape[0]
    low_shard = weights.astype(jnp.bfloat16)
    owner_grads = jnp.zeros(weights.shape, jnp.float32)
    vector_total = jnp.zeros(vectors.shape, jnp.float32)
    outputs = []
    input_grads = []
    for micro_index in range(micro_count):
        weight_stack = gather_weights(low_shard)
        output, grad_input, weight_grads, vector_grads = layer_pass(
            tokens[micro_index], cotangent[micro_index], weight_stack, vectors
        )
        outputs.append(output)
        input_grads.append(grad_input)
        vector_total = vector_total + vector_grads
        owner_grads = owner_grads + reduce_grads(weight_grads)
    vector_sum = lax.psum(vector_total, ("clip", "seq", "fsdp"))
    new_momentum = DECAY * momentum + owner_grads
    full_moment = lax.all_gather(
        new_momentum.astype(jnp.bfloat16), "seq", axis=1, tiled=True
    ).astype(new_momentum.dtype)
    whole_result = jax.vmap(newton_schulz)(full_moment)
    row_count = new_momentum.shape[1]
    orthogonal = lax.dynamic_slice_in_dim(
        whole_result, lax.axis_index("seq") * row_count, row_count, 1
    )
    local_count = weights.shape[0]
    matrix_index = lax.axis_index(("clip", "fsdp")) * local_count + jnp.arange(local_count)
    new_weights = weights - MUON_RATE * factor_of(matrix_index)[:, None, None] * orthogonal
    total_tokens = (
        micro_count * tokens.shape[1] * lax.axis_size(("clip", "fsdp")) * FRAMES * PATCHES
    )
    new_vectors = vectors - VECTOR_RATE * total_tokens ** (-0.5) * vector_sum
    return (
        jnp.stack(outputs),
        jnp.stack(input_grads),
        new_momentum,
        new_weights,
        new_weights.astype(jnp.bfloat16),
        vector_sum,
        new_vectors,
    )


def solution(mesh):
    in_specs = (
        P(None, ("clip", "fsdp"), "seq", None, None),
        P(None, ("clip", "fsdp"), "seq", None, None),
        P(("clip", "fsdp"), "seq", None),
        P(("clip", "fsdp"), "seq", None),
        P(),
    )
    out_specs = (
        P(None, ("clip", "fsdp"), "seq", None, None),
        P(None, ("clip", "fsdp"), "seq", None, None),
        P(("clip", "fsdp"), "seq", None),
        P(("clip", "fsdp"), "seq", None),
        P(("clip", "fsdp"), "seq", None),
        P(),
        P(),
    )
    return jax.shard_map(body, mesh=mesh, in_specs=in_specs, out_specs=out_specs, check_vma=False)
```

profile of v0, /device:TPU:0, one launch (start us, length us, event | category | flops | bytes accessed | tf_op | source)
XLA Modules:
  0.0 1405.3 jit_solution(8575568759892990669)
XLA Ops:
  9.6 26.0 %all-gather.4.cloned.1.call-done = bf16[1,768,768]{2,1,0:T(8,128)(2,1)} async-done(((bf16[1,384,768]{2,1,0:T(8,128)(2,1)}), bf16[1,768,768]{2,1,0:T(8,128)(2,1)}) %all-gather.4.cloned.1.call-update) | async-done | bytes 1179664 | tf_op jit(solution)/shard_map/all_gather | solution.py:338
  38.2 98.1 %all-gather.6.cloned.1.call-done = bf16[16,768,768]{2,1,0:T(8,128)(2,1)} async-done(((bf16[1,768,768]{2,1,0:T(8,128)(2,1)}), bf16[16,768,768]{2,1,0:T(8,128)(2,1)}) %all-gather.6.cloned.1.call-update) | async-done | bytes 18874384 | tf_op jit(solution)/shard_map/all_gather | solution.py:339
  212.0 10.3 all-to-all-done
  232.8 13.5 all-to-all-done.2
  270.5 8.0 multiply_reduce_fusion.6
  288.2 6.8 convert_bitcast_fusion.7
  298.0 6.2 convert_element_type.905
  326.4 8.0 multiply_reduce_fusion.4
  341.2 6.3 reshape.1708
  347.5 6.8 convert_bitcast_fusion.6
  382.7 10.6 all-to-all-done.3
  397.1 11.2 fusion.130
  408.4 20.6 %fusion.82 = (u8[128,4,768]{2,0,1:T(8,128)(4,1)S(1)}, u8[128,4,768]{2,0,1:T(8,128)(4,1)}, u8[128,4,768]{2,0,1:T(8,128)(4,1)}, u8[128,4,768]{2,0,1:T(8,128)(4,1)}, f32[8,128,4,768]{3,1,2,0:T(8,128)}) fusion(f32[4,768]{1,0:T(4,128)S(1)} %copy-done.108, f32[8,128,4,768]{3,1,2,0:T(8,128)} %fusion.130, bf16[16,768,768]{2,1,0:T(8,128)(2,1)} %all-gather.6.cloned.1.call-done, ...), kind=kOutput, calls=%fused_computation.229 | convolution fusion | flops 4922277888 | bytes 34631680 | tf_op jit(solution)/shard_map/cfpd,jde->cfpje/dot_general | solution.py:213
  429.0 62.4 %multiply_convert_fusion.1 = (bf16[8,128,4,768]{3,1,2,0:T(8,128)(2,1)}, f32[8,128,4,768]{3,1,2,0:T(8,128)}, bf16[8,128,4,768]{3,1,2,0:T(8,128)(2,1)}, f32[8,128,4,768]{3,1,2,0:T(8,128)}) fusion(f32[8,128,4,768]{3,1,2,0:T(8,128)} %get-tuple-element.111, f32[4,768]{1,0:T(4,128)S(1)} %copy-done.108, u8[128,4,768]{2,0,1:T(8,128)(4,1)} %get-tuple-element.22, ...), kind=kLoop, calls=%fused_computation.30 | loop fusion | flops 443547648 | bytes 64499712 | tf_op jit(solution)/shard_map/convert_element_type | solution.py:219
  491.4 17.4 %convert_reduce_fusion.1 = (f32[4,768]{1,0:T(4,128)}, bf16[8,128,4,768]{3,1,2,0:T(8,128)(2,1)}) fusion(f32[8,128,4,768]{3,1,2,0:T(8,128)} %get-tuple-element.77, bf16[16,768,768]{2,1,0:T(8,128)(2,1)} %all-gather.6.cloned.1.call-done, bf16[2,1,8,128,768]{4,3,2,1,0:T(8,128)(2,1)S(1)} %copy-done.31, f32[8,128,4,768]{3,1,2,0:T(8,128)} %get-tuple-element.111, ...), kind=kOutput, calls=%fused_computation.14 | convolution fusion | flops 4885312512 | bytes 37773312 | tf_op jit(solution)/shard_map/cfpd,jed->cfpje/dot_general | solution.py:231
  508.9 17.2 %convert_reduce_fusion = (f32[4,768]{1,0:T(4,128)}, bf16[8,128,4,768]{3,1,2,0:T(8,128)(2,1)}) fusion(f32[8,128,4,768]{3,1,2,0:T(8,128)} %get-tuple-element.85, bf16[16,768,768]{2,1,0:T(8,128)(2,1)} %all-gather.6.cloned.1.call-done, bf16[2,1,8,128,768]{4,3,2,1,0:T(8,128)(2,1)S(1)} %copy-done.31, f32[8,128,4,768]{3,1,2,0:T(8,128)} %fusion.130, ...), kind=kOutput, calls=%fused_computation.13 | convolution fusion | flops 4885312512 | bytes 37773312 | tf_op jit(solution)/shard_map/cfpd,jed->cfpje/dot_general | solution.py:231
  526.1 9.1 fusion.178
  535.3 11.1 fusion.75
  565.0 8.7 all-to-all-done.4
  585.1 6.2 reshape.1711
  591.3 13.1 multiply_reduce_fusion.3
  608.5 8.0 convert_reduce_fusion.5
  620.5 8.5 convert_reduce_fusion.4
  635.7 6.4 reshape.1713
  642.2 9.4 convert_reduce_fusion.2
  651.6 11.2 multiply_reduce_fusion.1
  670.8 7.9 convert_reduce_fusion.3
  681.8 6.2 convert_element_type.971
  691.0 6.2 convert_element_type.967
  700.3 6.4 convert_element_type.975
  748.1 6.5 convert_element_type.1004
  851.2 9.8 fusion.13
  861.0 7.1 fusion.14
  912.5 8.3 multiply_reduce_fusion
  974.3 9.9 fusion.16
  984.2 7.4 fusion.17
  994.3 9.5 fusion.156
  1003.8 8.6 fusion.157
  1014.3 49.4 %reduce-scatter.9.cloned.1.call-done = bf16[1,768,768]{1,2,0:T(8,128)(2,1)} async-done(((bf16[16,768,768]{1,2,0:T(8,128)(2,1)}), bf16[1,768,768]{1,2,0:T(8,128)(2,1)}) %reduce-scatter.9.cloned.1.call-update) | async-done | bytes 1179664 | tf_op jit(solution)/shard_map/reduce_scatter | solution.py:343
  1063.8 6.5 copy.392
  1098.9 162.9 %reduce-scatter.11.cloned.1.call-done = bf16[1,768,768]{1,2,0:T(8,128)(2,1)} async-done(((bf16[16,768,768]{1,2,0:T(8,128)(2,1)}), bf16[1,768,768]{1,2,0:T(8,128)(2,1)}) %reduce-scatter.11.cloned.1.call-update) | async-done | bytes 1179664 | tf_op jit(solution)/shard_map/reduce_scatter | solution.py:343
  1261.8 6.7 copy.394
  1271.9 8.7 fusion.49
  1284.8 39.8 %psum.7 = f32[17,768]{1,0:T(8,128)S(1)} all-reduce(f32[17,768]{1,0:T(8,128)S(1)} %add.572), channel_id=1, replica_groups=mesh['clip'=4,'seq'=2,'fsdp'=4] {'clip','seq','fsdp'}, use_global_device_ids=true, to_apply=%region_69.0 | all-reduce | flops 13056 | bytes 104448 | tf_op jit(solution)/shard_map/psum | solution.py:376
  1340.7 14.4 %all-gather.8.cloned.1.call-done = bf16[1,768,768]{2,1,0:T(8,128)(2,1)} async-done(((bf16[1,384,768]{2,1,0:T(8,128)(2,1)}), bf16[1,768,768]{2,1,0:T(8,128)(2,1)}) %all-gather.8.cloned.1.call-update) | async-done | bytes 1179664 | tf_op jit(solution)/shard_map/all_gather | solution.py:378
  1358.3 7.8 fusion.93
  1372.1 6.4 bitcast_add_fusion.4
  1384.4 6.2 fusion.242
  (599 shorter events, 564.2 us)
Async XLA Ops:
  7.2 28.5 %copy-start.94 = (f32[17,768]{1,0:T(8,128)S(1)}, f32[17,768]{1,0:T(8,128)}, u32[]{:S(2)}) copy-start(f32[17,768]{1,0:T(8,128)} %param.9) | copy-start | bytes 156676
  7.2 29.2 %copy-start.5 = (bf16[2,1,8,128,768]{4,3,2,1,0:T(8,128)(2,1)S(1)}, bf16[2,1,8,128,768]{4,3,2,1,0:T(8,128)(2,1)}, u32[]{:S(2)}) copy-start(bf16[2,1,8,128,768]{4,3,2,1,0:T(8,128)(2,1)} %param.5) | copy-start | bytes 9437188
  7.2 28.5 %all-gather.4.cloned.1.call-start = ((), (), s32[]{:S(2)}) async-start(), calls=%async_computation.12 | async-start | bytes 1769472 | tf_op jit(solution)/shard_map/all_gather | solution.py:338
  9.6 126.7 %all-gather.6.cloned.1.call-start = ((), (), s32[]{:S(2)}) async-start(), calls=%async_computation.13 | async-start | bytes 20054016 | tf_op jit(solution)/shard_map/all_gather | solution.py:339
  36.4 144.8 %copy-start.122 = (f32[768]{0:T(1024)}, f32[768]{0:T(1024)S(1)}, u32[]{:S(2)}) copy-start(f32[768]{0:T(1024)S(1)} %get-tuple-element.68) | copy-start | bytes 9220
  36.4 144.8 %copy-start.144 = (f32[768]{0:T(1024)}, f32[768]{0:T(1024)S(1)}, u32[]{:S(2)}) copy-start(f32[768]{0:T(1024)S(1)} %get-tuple-element.67) | copy-start | bytes 9220
  36.4 216.6 %copy-start.96 = (f32[768]{0:T(1024)}, f32[768]{0:T(1024)S(1)}, u32[]{:S(2)}) copy-start(f32[768]{0:T(1024)S(1)} %get-tuple-element.63) | copy-start | bytes 9220
  36.4 360.7 %copy-start.114 = (f32[768]{0:T(1024)}, f32[768]{0:T(1024)S(1)}, u32[]{:S(2)}) copy-start(f32[768]{0:T(1024)S(1)} %get-tuple-element.57) | copy-start | bytes 9220
  36.4 360.6 %copy-start.124 = (f32[768]{0:T(1024)}, f32[768]{0:T(1024)S(1)}, u32[]{:S(2)}) copy-start(f32[768]{0:T(1024)S(1)} %get-tuple-element.58) | copy-start | bytes 9220
  36.9 118.3 %copy-start.109 = (f32[8,128]{1,0:T(8,128)}, f32[8,128]{1,0:T(8,128)S(1)}, u32[]{:S(2)}) copy-start(f32[8,128]{1,0:T(8,128)S(1)} %get-tuple-element.143) | copy-start | bytes 12292
  36.9 144.2 %copy-start.111 = (f32[8,128]{1,0:T(8,128)}, f32[8,128]{1,0:T(8,128)S(1)}, u32[]{:S(2)}) copy-start(f32[8,128]{1,0:T(8,128)S(1)} %get-tuple-element.144) | copy-start | bytes 12292
  38.1 117.1 %copy-start.130 = (f32[8,128]{1,0:T(8,128)}, f32[8,128]{1,0:T(8,128)S(1)}, u32[]{:S(2)}) copy-start(f32[8,128]{1,0:T(8,128)S(1)} %add_rsqrt_fusion.4) | copy-start | bytes 12292
  38.2 143.0 %copy-start.132 = (f32[8,128]{1,0:T(8,128)}, f32[8,128]{1,0:T(8,128)S(1)}, u32[]{:S(2)}) copy-start(f32[8,128]{1,0:T(8,128)S(1)} %add_rsqrt_fusion.5) | copy-start | bytes 12292
  155.2 47.1 %copy-start.65 = (f32[8,12,128]{2,1,0:T(8,128)}, f32[8,12,128]{2,1,0:T(8,128)S(1)}, u32[]{:S(2)}) copy-start(f32[8,12,128]{2,1,0:T(8,128)S(1)} %log_add_fusion.2) | copy-start | bytes 147460
  197.7 24.6 %all-to-all-start = ((bf16[1,8,128,768]{3,1,0,2:T(8,128)(2,1)}), bf16[1,8,128,768]{3,1,0,2:T(8,128)(2,1)}, u32[]{:S(2)}, u32[]{:S(2)}) async-start(bf16[1,8,128,768]{3,1,0,2:T(8,128)(2,1)} %copy.243), calls=%async_computation | async-start | bytes 3145728 | tf_op jit(solution)/shard_map/all_to_all | solution.py:192
  222.3 24.0 %all-to-all-start.2 = ((bf16[1,8,128,768]{3,1,0,2:T(8,128)(2,1)}), bf16[1,8,128,768]{3,1,0,2:T(8,128)(2,1)}, u32[]{:S(2)}, u32[]{:S(2)}) async-start(bf16[1,8,128,768]{3,1,0,2:T(8,128)(2,1)} %copy.257), calls=%async_computation.2 | async-start | bytes 3145728 | tf_op jit(solution)/shard_map/all_to_all | solution.py:192
  252.9 122.2 %copy-start.98 = (f32[16,64]{1,0:T(8,128)}, f32[16,64]{1,0:T(8,128)S(1)}, u32[]{:S(2)}) copy-start(f32[16,64]{1,0:T(8,128)S(1)} %get-tuple-element.88) | copy-start | bytes 12292
  308.5 62.9 %all-to-all-start.1 = ((bf16[1,16,64,768]{3,2,0,1:T(8,128)(2,1)}), bf16[1,16,64,768]{3,2,0,1:T(8,128)(2,1)S(1)}, u32[]{:S(2)}, u32[]{:S(2)}) async-start(bf16[1,16,64,768]{3,2,0,1:T(8,128)(2,1)} %fusion.158), calls=%async_computation.1 | async-start | bytes 3145728 | tf_op jit(solution)/shard_map/all_to_all | solution.py:208
  337.2 10.3 copy-start.22
  371.5 21.8 %all-to-all-start.3 = ((bf16[1,16,64,768]{3,2,0,1:T(8,128)(2,1)}), bf16[1,16,64,768]{3,2,0,1:T(8,128)(2,1)S(1)}, u32[]{:S(2)}, u32[]{:S(2)}) async-start(bf16[1,16,64,768]{3,2,0,1:T(8,128)(2,1)} %fusion.159), calls=%async_computation.3 | async-start | bytes 3145728 | tf_op jit(solution)/shard_map/all_to_all | solution.py:208
  396.2 12.1 copy-start.136
  396.3 12.0 copy-start.100
  397.0 11.4 copy-start.102
  397.0 11.3 copy-start.139
  397.0 11.3 copy-start.34
  397.1 11.3 copy-start.108
  397.1 11.3 copy-start.135
  397.1 11.3 copy-start.138
  429.0 62.4 %copy-start.31 = (bf16[2,1,8,128,768]{4,3,2,1,0:T(8,128)(2,1)S(1)}, bf16[2,1,8,128,768]{4,3,2,1,0:T(8,128)(2,1)}, u32[]{:S(2)}) copy-start(bf16[2,1,8,128,768]{4,3,2,1,0:T(8,128)(2,1)} %param.6) | copy-start | bytes 9437188
  551.8 21.9 %all-to-all-start.4 = ((bf16[1,8,128,768]{3,1,0,2:T(8,128)(2,1)}), bf16[1,8,128,768]{3,1,0,2:T(8,128)(2,1)}, u32[]{:S(2)}, u32[]{:S(2)}) async-start(bf16[1,8,128,768]{3,1,0,2:T(8,128)(2,1)} %copy.266), calls=%async_computation.4 | async-start | bytes 3145728 | tf_op jit(solution)/shard_map/all_to_all | solution.py:246
  573.7 55.3 %all-to-all-start.6 = ((bf16[1,8,128,768]{3,1,0,2:T(8,128)(2,1)}), bf16[1,8,128,768]{3,1,0,2:T(8,128)(2,1)}, u32[]{:S(2)}, u32[]{:S(2)}) async-start(bf16[1,8,128,768]{3,1,0,2:T(8,128)(2,1)} %copy.286), calls=%async_computation.6 | async-start | bytes 3145728 | tf_op jit(solution)/shard_map/all_to_all | solution.py:246
  585.1 19.3 %slice-start.4 = ((s8[6291456]{0:T(1024)(128)(4,1)}), s8[2097152]{0:T(1024)(128)(4,1)S(1)}, s32[]{:S(2)}) async-start(s8[6291456]{0:T(1024)(128)(4,1)} %bitcast.738), calls=%async_computation.23 | async-start | bytes 4194304
  591.3 13.1 slice-start.5
  635.7 15.9 %slice-start.6 = ((s8[6291456]{0:T(1024)(128)(4,1)}), s8[2097152]{0:T(1024)(128)(4,1)S(1)}, s32[]{:S(2)}) async-start(s8[6291456]{0:T(1024)(128)(4,1)} %bitcast.740), calls=%async_computation.25 | async-start | bytes 4194304
  768.2 21.2 %all-to-all-start.5 = ((bf16[1,16,64,768]{3,2,0,1:T(8,128)(2,1)}), bf16[1,16,64,768]{3,2,0,1:T(8,128)(2,1)S(1)}, u32[]{:S(2)}, u32[]{:S(2)}) async-start(bf16[1,16,64,768]{3,2,0,1:T(8,128)(2,1)} %get-tuple-element.98), calls=%async_computation.5 | async-start | bytes 3145728 | tf_op jit(solution)/shard_map/all_to_all | solution.py:269
  772.0 291.8 %reduce-scatter.9.cloned.1.call-start = ((), (), s32[]{:S(2)}) async-start(), calls=%async_computation.14 | async-start | bytes 20054016 | tf_op jit(solution)/shard_map/reduce_scatter | solution.py:343
  847.8 13.2 slice-start.10
  873.6 29.6 %all-to-all-start.7 = ((bf16[1,16,64,768]{3,2,0,1:T(8,128)(2,1)}), bf16[1,16,64,768]{3,2,0,1:T(8,128)(2,1)}, u32[]{:S(2)}, u32[]{:S(2)}) async-start(bf16[1,16,64,768]{3,2,0,1:T(8,128)(2,1)} %fusion.135), calls=%async_computation.7 | async-start | bytes 3145728 | tf_op jit(solution)/shard_map/all_to_all | solution.py:269
  878.3 383.5 %reduce-scatter.11.cloned.1.call-start = ((), (), s32[]{:S(2)}) async-start(), calls=%async_computation.15 | async-start | bytes 20054016 | tf_op jit(solution)/shard_map/reduce_scatter | solution.py:343
  971.0 13.2 slice-start.8
  974.3 9.9 copy-start.33
  974.3 9.9 slice-start.9
  991.7 333.0 %reduce-scatter.13.cloned.1.call-start = ((), (), s32[]{:S(2)}) async-start(), calls=%async_computation.17 | async-start | bytes 1769472
  1073.2 254.2 %reduce-scatter.15.cloned.1.call-start = ((), (), s32[]{:S(2)}) async-start(), calls=%async_computation.18 | async-start | bytes 1769472
  1271.8 10.7 copy-start.116
  1271.8 10.7 copy-start.121
  1271.8 83.3 %all-gather.8.cloned.1.call-start = ((), (), s32[]{:S(2)}) async-start(), calls=%async_computation.16 | async-start | bytes 1769472 | tf_op jit(solution)/shard_map/all_gather | solution.py:378
  1324.6 15.5 %copy-start.93 = (f32[17,768]{1,0:T(8,128)}, f32[17,768]{1,0:T(8,128)S(1)}, u32[]{:S(2)}) copy-start(f32[17,768]{1,0:T(8,128)S(1)} %psum.7) | copy-start | bytes 156676
  (129 other events, 548.4 us)
Sparse Core Ops, SparseCore 0:
  10.1 25.4 all-gather.3
  37.2 98.9 all-gather.5
  868.3 195.4 reduce-scatter.8
  1067.7 194.0 reduce-scatter.10
  1264.5 20.8 reduce-scatter.12
  1288.1 21.9 reduce-scatter.14
  1332.4 22.6 all-gather.7
where the time goes:
time: 1420 us; the launch traced here: 1410 us
  matrix products  501 us (35%)
  waiting for transfers between devices  394 us (28%)
  local copies, waits for them, and re-layouts  265 us (19%)
  other arithmetic  153 us (11%)
  blocking collectives  39.8 us (3%)
  starting transfers between devices  35 us (2%)
  between operations  17.3 us (1%)
    reduce_scatter x2, waiting for transfers between devices, reduce_grads(): lax.psum_scatter(weight_grads.astype(jnp.bfloat16), ('clip', 'fsdp'), sca...  212 us
    all_gather x1, waiting for transfers between devices, gather_weights(): return lax.all_gather(row_full, ('clip', 'fsdp'), axis=0, tiled=True)  98.1 us
    dot_general x16, matrix products, multiply_back(): jnp.einsum('...e,de->...d', grads, matrix, preferred_element_type=jnp.flo...  65.7 us
    convert_element_type x1, other arithmetic, layer_pass(): active_low = activated.astype(jnp.bfloat16)  62.4 us
    unnamed x346, local copies, waits for them, and re-layouts  60.9 us
    dot_general x16, matrix products, multiply(): jnp.einsum('...d,de->...e', values, matrix, preferred_element_type=jnp.fl...  59.1 us
    dot_general x16, matrix products, outer_sum(): jnp.einsum('...d,...e->de', values, grads, preferred_element_type=jnp.flo...  53.9 us
    psum x1, blocking collectives, body(): vector_sum = lax.psum(vector_total, ('clip', 'seq', 'fsdp'))  39.8 us
  transfers between devices with their start and end apart: 15, of which 9 were waited for; matrix products, arithmetic and copies ran while one was open for 26% of the time, Pallas kernels for 0%

commit v1 on v0

--- a/solution.py
+++ b/solution.py
@@ -1,6 +1,11 @@
+import functools
+import math
+
 import jax
 import jax.numpy as jnp
 from jax import lax
+from jax.experimental import pallas as pl
+from jax.experimental.pallas import tpu as pltpu
 from jax.sharding import PartitionSpec as P
 
 HEADS = 12
@@ -401,6 +406,1666 @@
     )
 
 
+BF16 = jnp.bfloat16
+F32 = jnp.float32
+TILE = 512
+BLOCK = 128
+PAIRS = HEADS // 2
+LOG2E = 1.4426950408889634
+VMEM_LIMIT = 60 * 1024 * 1024
+MESH = pl.DeviceIdType.MESH
+
+
+def dot(left, right, left_dim=1, right_dim=0):
+    return lax.dot_general(
+        left, right, (((left_dim,), (right_dim,)), ((), ())), preferred_element_type=F32
+    )
+
+
+def row_stats(values):
+    average = jnp.mean(values, -1, keepdims=True)
+    centred = values - average
+    inverse = lax.rsqrt(jnp.mean(centred * centred, -1, keepdims=True) + EPS_NORM)
+    return centred * inverse, inverse
+
+
+def norm_pull(grads, normal, inverse, gain_row):
+    scaled = grads * gain_row
+    return inverse * (
+        scaled
+        - jnp.mean(scaled, -1, keepdims=True)
+        - normal * jnp.mean(scaled * normal, -1, keepdims=True)
+    )
+
+
+def column_sum(values):
+    return jnp.sum(values.astype(F32), 0, keepdims=True)
+
+
+def load_rows(ref, temporal):
+    values = ref[...].astype(F32)
+    if not temporal:
+        return values
+    frames, places, width = values.shape
+    values = values.reshape(frames, places // 8, 8, width)
+    return values.transpose(1, 0, 2, 3).reshape(frames * places, width)
+
+
+def store_rows(ref, values, temporal):
+    if temporal:
+        frames, places, width = ref.shape
+        values = values.reshape(places // 8, frames, 8, width)
+        values = values.transpose(1, 0, 2, 3).reshape(frames, places, width)
+    ref[...] = values.astype(ref.dtype)
+
+
+def half_masks():
+    lane = lax.broadcasted_iota(jnp.int32, (1, BLOCK), 1)
+    low = (lane < HEAD).astype(F32)
+    return low.astype(BF16), (1.0 - low).astype(BF16)
+
+
+def stacked(values, masks):
+    return jnp.concatenate([values * masks[0], values * masks[1]], 0)
+
+
+def place_mask():
+    rows = lax.broadcasted_iota(jnp.int32, (BLOCK, BLOCK), 0)
+    columns = lax.broadcasted_iota(jnp.int32, (BLOCK, BLOCK), 1)
+    same = lax.rem(rows, 8) == lax.rem(columns, 8)
+    return jnp.concatenate([same, same], 1)
+
+
+def head_sums():
+    rows = lax.broadcasted_iota(jnp.int32, (2 * BLOCK, BLOCK), 0)
+    lanes = lax.broadcasted_iota(jnp.int32, (2 * BLOCK, BLOCK), 1)
+    return ((rows < BLOCK) == (lanes < HEAD)).astype(F32).astype(BF16)
+
+
+def lane_pairs():
+    return [slice(pair * BLOCK, (pair + 1) * BLOCK) for pair in range(PAIRS)]
+
+
+def powers_of(scores, mask):
+    if mask is not None:
+        scores = jnp.where(mask, scores, -1e30)
+    parts = []
+    for side in range(2):
+        half = scores[:, side * BLOCK : (side + 1) * BLOCK]
+        top = jnp.max(half, -1, keepdims=True)
+        parts.append(jnp.exp2((half - top) * (LOG2E * HEAD ** (-0.5))).astype(BF16))
+    return jnp.concatenate(parts, 1)
+
+
+ERF_P = 0.3275911
+ERF_A = (0.254829592, -0.284496736, 1.421413741, -1.453152027, 1.061405429)
+BELL = (0.5 / math.pi) ** 0.5
+
+
+def gelu_pair(values):
+    bell = jnp.exp2(values * values * (-0.5 * LOG2E))
+    ratio = 1.0 / (1.0 + jnp.abs(values) * (ERF_P * 0.5 ** 0.5))
+    tail = 0.5 * ERF_A[4]
+    for term in ERF_A[3::-1]:
+        tail = tail * ratio + 0.5 * term
+    tail = tail * ratio * bell
+    cumulative = jnp.where(values < 0.0, tail, 1.0 - tail)
+    return values * cumulative, cumulative + values * bell * BELL
+
+
+def feed_kernel(
+    x_ref, vec_ref, w_ref, c_ref, part_ref,
+    y_ref, dx_ref, dup_ref, ddown_ref, dvec_ref, mixed_ref,
+    g_all, h_ref, z_ref, du_ref, y_acc, dh_acc, y_keep, blocks, sends, gots, loads,
+):
+    chunk = pl.program_id(0)
+    chunks = pl.num_programs(0)
+    step = pl.program_id(1)
+    steps = pl.num_programs(1)
+    tile = lax.rem(step + jnp.where(chunk == chunks - 1, steps // 2, 0), steps)
+    rows = pl.ds(pl.multiple_of(tile * TILE, TILE), TILE)
+    per_tile = TILE // BLOCK
+    mid = g_all.shape[0] // 2
+    quarter = mid // 2
+    side, depth, line, core = places()
+    chunk_line = lax.rem(line + chunk // 2, 2)
+    chunk_core = lax.rem(core + lax.rem(chunk, 2), 2)
+    hidden_block = 2 * chunk_line + chunk_core
+    width = x_ref.shape[1]
+    own = [pltpu.make_async_copy(w_ref.at[2 + u, line, core], blocks.at[u, 0], loads.at[u]) for u in range(2)]
+    across = pltpu.make_async_copy(
+        w_ref.at[2, 1 - line, core, side], blocks.at[0, 2, side], loads.at[2]
+    )
+    near = [
+        remote(blocks.at[u, 0], blocks.at[u, 1], sends.at[u], gots.at[u], other_core())
+        for u in range(2)
+    ]
+    far = [
+        remote(
+            blocks.at[0, 0, 1 - side], blocks.at[0, 2, 1 - side], sends.at[2], gots.at[2], other_line()
+        ),
+        remote(blocks.at[1, 0], blocks.at[1, 2], sends.at[3], gots.at[3], other_line()),
+    ]
+    cross = [
+        remote(blocks.at[u, 2], blocks.at[u, 3], sends.at[4 + u], gots.at[4 + u], other_core())
+        for u in range(2)
+    ]
+
+    g_own = pltpu.make_async_copy(c_ref.at[side], g_all.at[pl.ds(0, mid)], loads.at[3])
+    early = mid - mid // 4
+    g_part = pltpu.make_async_copy(part_ref.at[pl.ds(0, early)], g_all.at[pl.ds(mid, early)], loads.at[4])
+    g_move = remote(
+        c_ref.at[1 - side, pl.ds(early, mid - early)], g_all.at[pl.ds(mid + early, mid - early)],
+        sends.at[7], gots.at[7], other_side(),
+    )
+
+    @pl.when((chunk == 0) & (step == 3))
+    def _():
+        g_move.wait()
+
+    @pl.when((chunk == 0) & (step == 2))
+    def _():
+        g_part.wait()
+
+    @pl.when((chunk == 0) & (step == 0))
+    def _():
+        greet([other_core(), other_line(), other_side()])
+        for copy in own:
+            copy.start()
+        g_move.start()
+        g_own.start()
+        for copy in own:
+            copy.wait()
+        for copy in far + near:
+            copy.start()
+        across.start()
+        g_part.start()
+        g_own.wait()
+
+    @pl.when((chunk == 1) & (step == 0))
+    def _():
+        for copy in near:
+            copy.wait_recv()
+
+    @pl.when((chunk == 2) & (step == 0))
+    def _():
+        across.wait()
+        for copy in far:
+            copy.wait_recv()
+        for copy in cross:
+            copy.start()
+
+    @pl.when((chunk == 3) & (step == 0))
+    def _():
+        for copy in cross:
+            copy.wait_recv()
+
+    y_move = remote(
+        y_keep, mixed_ref.at[pl.ds(0, TILE // BLOCK)], sends.at[6], gots.at[6], other_side()
+    )
+
+    def block(which):
+        return blocks[which, chunk].reshape(width, width)
+
+    def grad_rows():
+        return g_all[pl.ds(tile * per_tile, per_tile)].reshape(TILE, width)
+
+    @pl.when(chunk == 0)
+    def _():
+        normal, inverse = row_stats(x_ref[rows, :].astype(F32))
+        h_ref[rows, :] = (normal * vec_ref[2:3] + vec_ref[5:6]).astype(BF16)
+        y_acc[rows, :] = jnp.zeros((TILE, x_ref.shape[1]), F32)
+        dh_acc[rows, :] = jnp.zeros((TILE, x_ref.shape[1]), F32)
+
+    @pl.when((chunk == 0) & (step == 0))
+    def _():
+        dvec_ref[...] = jnp.zeros_like(dvec_ref)
+
+    hidden = dot(h_ref[rows, :], block(0)) + vec_ref[pl.ds(13 + hidden_block, 1)]
+    grad_z = dot(grad_rows(), block(1), 1, 1)
+    active, slope = gelu_pair(hidden)
+    active_low = active.astype(BF16)
+    grad_u = (grad_z * slope).astype(BF16)
+    z_ref[rows, :] = active_low
+    du_ref[rows, :] = grad_u
+    y_acc[rows, :] += dot(active_low, block(1))
+    dh_acc[rows, :] += dot(grad_u, block(0), 1, 1)
+
+    @pl.when(step == steps - 1)
+    def _():
+        ddown_ref[0] = dot(z_ref[...], g_all[...].reshape(z_ref.shape), 0, 0).astype(BF16)
+        dup_ref[0] = dot(h_ref[...], du_ref[...], 0, 0).astype(BF16)
+        dvec_ref[pl.ds(3 + hidden_block, 1)] = column_sum(du_ref[...])
+
+    @pl.when(chunk == chunks - 1)
+    def _():
+        start = x_ref[rows, :].astype(F32)
+        result = (start + y_acc[rows, :] + vec_ref[12:13]).astype(BF16)
+        y_ref[...] = result
+
+        @pl.when(step == 0)
+        def _():
+            y_keep[...] = result[:TILE].reshape(y_keep.shape)
+            y_move.start()
+
+        normal, inverse = row_stats(start)
+        grad_normed = dh_acc[rows, :]
+        incoming = grad_rows().astype(F32)
+        back = norm_pull(grad_normed, normal, inverse, vec_ref[2:3])
+        dx_ref[...] = (incoming + back).astype(BF16)
+        dvec_ref[0:1] += column_sum(grad_normed * normal)
+        dvec_ref[1:2] += column_sum(grad_normed)
+        dvec_ref[2:3] += column_sum(incoming)
+
+    @pl.when((chunk == chunks - 1) & (step == steps - 1))
+    def _():
+        for copy in near + cross + far:
+            copy.wait_send()
+        y_move.wait()
+
+
+def feed(x, cotangent, grad_part, weight_stack, vectors):
+    tokens, width = x.shape
+    steps = tokens // TILE
+    chunks = 4
+    whole = pl.BlockSpec((tokens, width), lambda j, i: (0, 0), pipeline_mode=pl.Buffered(1))
+    last = pl.BlockSpec(
+        (TILE, width), lambda j, i: (lax.rem(jnp.where(j == chunks - 1, i, 0) + steps // 2, steps), 0)
+    )
+    weight_out = pl.BlockSpec((1, width, width), lambda j, i: (j, 0, 0))
+    dma = pltpu.SemaphoreType.DMA
+    return pl.pallas_call(
+        feed_kernel,
+        grid=(chunks, steps),
+        in_specs=[
+            whole,
+            pl.BlockSpec(vectors.shape, lambda j, i: (0, 0)),
+        ]
+        + [pl.BlockSpec(memory_space=pl.ANY)] * 3,
+        out_specs=[
+            last,
+            last,
+            weight_out,
+            weight_out,
+            pl.BlockSpec((8, width), lambda j, i: (0, 0)),
+            pl.BlockSpec(memory_space=pl.ANY),
+        ],
+        out_shape=[
+            jax.ShapeDtypeStruct((tokens, width), BF16),
+            jax.ShapeDtypeStruct((tokens, width), BF16),
+            jax.ShapeDtypeStruct((chunks, width, width), BF16),
+            jax.ShapeDtypeStruct((chunks, width, width), BF16),
+            jax.ShapeDtypeStruct((8, width), F32),
+            jax.ShapeDtypeStruct((tokens // BLOCK // 2, BLOCK, width), BF16),
+        ],
+        scratch_shapes=[pltpu.VMEM((tokens // BLOCK, BLOCK, width), BF16)]
+        + [pltpu.VMEM((tokens, width), BF16)] * 3
+        + [pltpu.VMEM((tokens, width), F32)] * 2
+        + [pltpu.VMEM((TILE // BLOCK, BLOCK, width), BF16)]
+        + [pltpu.VMEM((2, chunks) + weight_stack.shape[3:], BF16), dma((8,)), dma((8,)), dma((6,))],
+        compiler_params=pltpu.CompilerParams(
+            vmem_limit_bytes=VMEM_LIMIT, collective_id=5, has_side_effects=True
+        ),
+        name="feed",
+    )(x, vectors, weight_stack, cotangent, grad_part)
+
+
+def places():
+    side = lax.axis_index("seq")
+    depth = lax.axis_index("clip")
+    spot = lax.axis_index("fsdp")
+    core = lax.rem(spot, 2)
+    return side, depth, spot // 2, core
+
+
+def other_core():
+    _, _, line, core = places()
+    return {"fsdp": 2 * line + 1 - core}
+
+
+def other_side():
+    return {"seq": 1 - lax.axis_index("seq")}
+
+
+def other_line():
+    _, _, line, core = places()
+    return {"fsdp": 2 * (1 - line) + core}
+
+
+def other_depth(step):
+    return {"clip": lax.rem(lax.axis_index("clip") + step, lax.axis_size("clip"))}
+
+
+def greet(devices):
+    barrier = pltpu.get_barrier_semaphore()
+    for device in devices:
+        pl.semaphore_signal(barrier, inc=1, device_id=device, device_id_type=MESH)
+    pl.semaphore_wait(barrier, len(devices))
+
+
+def remote(source, target, send_sem, receive_sem, device):
+    return pltpu.make_async_remote_copy(
+        src_ref=source,
+        dst_ref=target,
+        send_sem=send_sem,
+        recv_sem=receive_sem,
+        device_id=device,
+        device_id_type=MESH,
+    )
+
+
+def add_rows(target, source, count, rows=96):
+    def one(index, carry):
+        place = pl.ds(pl.multiple_of(index * rows, rows), rows)
+        total = target[place, :].astype(F32) + source[place, :].astype(F32)
+        target[place, :] = total.astype(target.dtype)
+        return carry
+
+    lax.fori_loop(0, count // rows, one, 0)
+
+
+def attend_back_tile(
+    temporal, step, x_ref, d_ref, w_ref, vec_ref, q_ref, k_ref, v_ref, p_ref, o_ref, r_ref,
+    dvec_ref, dq_ref, dk_ref, dv_ref, do_ref, acc_ref, between, after=None,
+):
+    first = 1 if temporal else 0
+    masks = half_masks()
+
+    @pl.when(step == 0)
+    def _():
+        acc_ref[...] = jnp.zeros_like(acc_ref)
+        dvec_ref[...] = jnp.zeros_like(dvec_ref)
+
+    incoming = load_rows(d_ref, temporal)
+    incoming_low = incoming.astype(BF16)
+    do_ref[...] = (dot(incoming_low, w_ref[3], 1, 1) * r_ref[...]).astype(BF16)
+    acc_ref[3] += dot(o_ref[...], incoming_low, 0, 0)
+    sums = head_sums()
+    scale = HEAD ** (-0.5)
+
+    def one_block(block, carry):
+        rows = pl.ds(pl.multiple_of(block * BLOCK, BLOCK), BLOCK)
+        pairs = lane_pairs()
+        shifted = []
+        for lanes in pairs:
+            grad_o = do_ref[rows, lanes]
+            against = -(grad_o.astype(F32) * o_ref[rows, lanes].astype(F32))
+            shifted.append(
+                dot(
+                    jnp.concatenate([grad_o, against.astype(BF16)], 1),
+                    jnp.concatenate([stacked(v_ref[rows, lanes], masks), sums], 1),
+                    1,
+                    1,
+                )
+            )
+        turned = []
+        for pair in range(PAIRS):
+            low = p_ref[block, pair]
+            turned.append(jnp.concatenate([low[:, :BLOCK].T, low[:, BLOCK:].T], 1))
+        for pair, lanes in enumerate(pairs):
+            dv_ref[rows, lanes] = dot(turned[pair], stacked(do_ref[rows, lanes], masks)).astype(BF16)
+        scores = [
+            (p_ref[block, pair].astype(F32) * shifted[pair]).astype(BF16) for pair in range(PAIRS)
+        ]
+        turned = [
+            jnp.concatenate([score[:, :BLOCK].T, score[:, BLOCK:].T], 1) for score in scores
+        ]
+        for pair, lanes in enumerate(pairs):
+            dq_ref[rows, lanes] = (
+                dot(scores[pair], stacked(k_ref[rows, lanes], masks)) * scale
+            ).astype(BF16)
+        for pair, lanes in enumerate(pairs):
+            dk_ref[rows, lanes] = (
+                dot(turned[pair], stacked(q_ref[rows, lanes], masks)) * scale
+            ).astype(BF16)
+        return carry
+
+    lax.fori_loop(0, TILE // BLOCK, one_block, 0)
+    between()
+    normal, inverse = row_stats(load_rows(x_ref, temporal))
+    gain_row = vec_ref[first : first + 1]
+    normed = (normal * gain_row + vec_ref[first + 3 : first + 4]).astype(BF16)
+    acc_ref[0] += dot(normed, dq_ref[...], 0, 0)
+    acc_ref[1] += dot(normed, dk_ref[...], 0, 0)
+    acc_ref[2] += dot(normed, dv_ref[...], 0, 0)
+    if after is not None:
+        after()
+    grad_normed = (
+        dot(dq_ref[...], w_ref[0], 1, 1)
+        + dot(dk_ref[...], w_ref[1], 1, 1)
+        + dot(dv_ref[...], w_ref[2], 1, 1)
+    )
+    dvec_ref[0:1] += column_sum(grad_normed * normal)
+    dvec_ref[1:2] += column_sum(grad_normed)
+    dvec_ref[2:3] += column_sum(dq_ref[...])
+    dvec_ref[3:4] += column_sum(dv_ref[...])
+    dvec_ref[4:5] += column_sum(incoming)
+    return load_rows(d_ref, temporal) + norm_pull(grad_normed, normal, inverse, gain_row)
+
+
+def split_sum(
+    relative, source, near, local, from_x1, from_y1, from_x2, from_y2, sends, gots, loads, part=None
+):
+    side, depth, line, core = places()
+    if relative:
+        line, core = 0, 0
+    rows, width = local.shape[2:]
+    left = slice(0, width // 2)
+    right = slice(width // 2, width)
+    if part is None:
+        load = pltpu.make_async_copy(source.at[:, core], local, loads)
+        cores = [
+            remote(
+                source.at[y, 1 - core, x], near.at[y, x],
+                sends.at[5 + 2 * y + x], gots.at[5 + 2 * y + x], other_core(),
+            )
+            for y in range(2)
+            for x in range(2)
+        ]
+    else:
+        load = pltpu.make_async_copy(source.at[:, :, part], local, loads)
+        cores = []
+    one_x = remote(local.at[:, 1 - side, :, left], from_x1, sends.at[1], gots.at[1], other_side())
+    one_y = remote(local.at[1 - line, :, :, right], from_y1, sends.at[2], gots.at[2], other_line())
+    two_y = remote(local.at[1 - line, side, :, left], from_y2, sends.at[3], gots.at[3], other_line())
+    two_x = remote(local.at[line, 1 - side, :, right], from_x2, sends.at[4], gots.at[4], other_side())
+
+    def start():
+        for copy in cores:
+            copy.start()
+        load.start()
+
+    def stage_one():
+        load.wait()
+        for copy in cores:
+            copy.wait_recv()
+        if cores:
+            for y in range(2):
+                for x in range(2):
+                    add_rows(local.at[y, x], near.at[y, x], rows)
+        one_x.start()
+        one_y.start()
+
+    def stage_two():
+        one_x.wait_recv()
+        one_y.wait_recv()
+        for y in range(2):
+            add_rows(local.at[y, side, :, left], from_x1.at[y], rows)
+        for x in range(2):
+            add_rows(local.at[line, x, :, right], from_y1.at[x], rows)
+        two_y.start()
+        two_x.start()
+
+    def finish(result):
+        two_y.wait_recv()
+        two_x.wait_recv()
+        add_rows(from_y2, local.at[line, side, :, left], rows)
+        add_rows(from_x2, local.at[line, side, :, right], rows)
+        result[:, left] = from_y2[...]
+        result[:, right] = from_x2[...]
+
+    def close():
+        for copy in cores + [one_x, one_y, two_y, two_x]:
+            copy.wait_send()
+
+    return start, stage_one, stage_two, finish, close
+
+
+def split_scratch(rows, width, near=True):
+    half = width // 2
+    return [
+        pltpu.VMEM((2, 2, rows, width) if near else (16, width), BF16),
+        pltpu.VMEM((2, 2, rows, width), BF16),
+        pltpu.VMEM((2, rows, half), BF16),
+        pltpu.VMEM((2, rows, half), BF16),
+        pltpu.VMEM((rows, half), BF16),
+        pltpu.VMEM((rows, half), BF16),
+        pltpu.SemaphoreType.DMA((9,)),
+        pltpu.SemaphoreType.DMA((9,)),
+        pltpu.SemaphoreType.DMA,
+    ]
+
+
+def line_sum(relative, source, near, local, from_y, from_x, sends, gots, loads):
+    side, depth, line, core = places()
+    if relative:
+        line, core = 0, 0
+    rows = local.shape[2]
+    load = pltpu.make_async_copy(source.at[:, core], local, loads)
+    cores = [
+        remote(
+            source.at[y, 1 - core, x], near.at[y, x],
+            sends.at[4 + 2 * y + x], gots.at[4 + 2 * y + x], other_core(),
+        )
+        for y in range(2)
+        for x in range(2)
+    ]
+    lines = [
+        remote(local.at[1 - line, x], from_y.at[x], sends.at[1 + k], gots.at[1 + k], other_line())
+        for k, x in enumerate((1 - side, side))
+    ]
+    sides = remote(local.at[line, 1 - side], from_x, sends.at[3], gots.at[3], other_side())
+
+    def start():
+        for copy in cores:
+            copy.start()
+        load.start()
+
+    def stage_one():
+        load.wait()
+        for copy in cores:
+            copy.wait_recv()
+        for y in range(2):
+            for x in range(2):
+                add_rows(local.at[y, x], near.at[y, x], rows)
+        for copy in lines:
+            copy.start()
+
+    def stage_two():
+        lines[0].wait_recv()
+        add_rows(local.at[line, 1 - side], from_y.at[1 - side], rows)
+        sides.start()
+
+    def finish(result):
+        lines[1].wait_recv()
+        add_rows(local.at[line, side], from_y.at[side], rows)
+        sides.wait_recv()
+        add_rows(from_x, local.at[line, side], rows)
+        result[...] = from_x[...]
+
+    def close():
+        for copy in cores + [sides] + lines:
+            copy.wait_send()
+
+    return start, stage_one, stage_two, finish, close
+
+
+def line_scratch(rows, width):
+    return [
+        pltpu.VMEM((2, 2, rows, width), BF16),
+        pltpu.VMEM((2, 2, rows, width), BF16),
+        pltpu.VMEM((2, rows, width), BF16),
+        pltpu.VMEM((rows, width), BF16),
+        pltpu.SemaphoreType.DMA((8,)),
+        pltpu.SemaphoreType.DMA((8,)),
+        pltpu.SemaphoreType.DMA,
+    ]
+
+
+def depth_sum(owner, total, from_q, parts, q_sends, q_gots, b_sends, b_gots):
+    depth = lax.axis_index("clip")
+    depths = lax.axis_size("clip")
+    share = total.shape[0] // depths
+
+    def rows_of(z):
+        return pl.ds(pl.multiple_of(z * share, share), share)
+
+    def spread(step):
+        to = lax.rem(depth + step, depths)
+        return remote(
+            total.at[rows_of(to)], from_q.at[step - 1], q_sends.at[step - 1], q_gots.at[step - 1], {"clip": to}
+        )
+
+    collect = remote(parts.at[rows_of(depth)], parts.at[rows_of(depth)], b_sends, b_gots.at[depth], {"clip": owner})
+
+    def start():
+        for step in range(1, depths):
+            spread(step).start()
+
+    def gather():
+        for step in range(1, depths):
+            spread(step).wait_recv()
+        summed = total[rows_of(depth), :].astype(F32)
+        for step in range(1, depths):
+            summed = summed + from_q[step - 1].astype(F32)
+        parts[rows_of(depth), :] = summed.astype(BF16)
+
+        @pl.when(depth != owner)
+        def _():
+            collect.start()
+
+    def finish():
+        @pl.when(depth == owner)
+        def _():
+            for z in range(depths):
+                if z != owner:
+                    place = parts.at[rows_of(z)]
+                    remote(place, place, b_sends, b_gots.at[z], other_core()).wait_recv()
+
+    def close():
+        for step in range(1, depths):
+            spread(step).wait_send()
+
+        @pl.when(depth != owner)
+        def _():
+            collect.wait_send()
+
+    return start, gather, finish, close
+
+
+def depth_scratch(half, width):
+    depths = lax.axis_size("clip")
+    dma = pltpu.SemaphoreType.DMA
+    return [
+        pltpu.VMEM((depths - 1, half // depths, width), BF16),
+        pltpu.VMEM((half, width), BF16),
+        dma((depths - 1,)),
+        dma((depths - 1,)),
+        dma,
+        dma((depths,)),
+    ]
+
+
+SPLIT = 9
+
+
+LINE = 7
+DEPTH = 6
+
+
+def back_two_kernel(
+    x_ref, d_ref, w_ref, vec_ref, q_ref, k_ref, v_ref, p_ref, o_ref, r_ref, up_ref, down_ref,
+    dx_ref, dw_ref, dvec_ref, up_out, down_out,
+    dq_ref, dk_ref, dv_ref, do_ref, acc_ref, *sums,
+):
+    step = pl.program_id(0)
+    side, depth, line, core = places()
+    up = split_sum(True, up_ref, *sums[:SPLIT])
+    down = split_sum(True, down_ref, *sums[SPLIT:])
+    @pl.when(step == 0)
+    def _():
+        greet([other_core(), other_side(), other_line()])
+        up[0]()
+
+    @pl.when(step == 3)
+    def _():
+        down[2]()
+
+    def between():
+        @pl.when(step == 0)
+        def _():
+            up[1]()
+            down[0]()
+
+        @pl.when(step == 1)
+        def _():
+            down[1]()
+
+        @pl.when(step == 2)
+        def _():
+            up[2]()
+
+    result = attend_back_tile(
+        True, step, x_ref, d_ref, w_ref, vec_ref, q_ref, k_ref, v_ref, p_ref, o_ref, r_ref,
+        dvec_ref, dq_ref, dk_ref, dv_ref, do_ref, acc_ref, between,
+    )
+    store_rows(dx_ref, result, True)
+
+    @pl.when(step == pl.num_programs(0) - 1)
+    def _():
+        up[3](up_out)
+        down[3](down_out)
+        up[4]()
+        down[4]()
+        dw_ref[...] = acc_ref[...].astype(BF16).reshape(dw_ref.shape)
+
+
+def back_specs(full, vectors, at, rows_at, group):
+    frames, patches, width = full
+    rows = pl.BlockSpec((TILE, width), lambda i: (rows_at(i), 0))
+    chances = pl.BlockSpec((TILE // BLOCK, PAIRS, BLOCK, 2 * BLOCK), lambda i: (rows_at(i), 0, 0, 0))
+    return [
+        at,
+        at,
+        pl.BlockSpec((4, width, width), lambda i: (group, 0, 0), pipeline_mode=pl.Buffered(1)),
+        pl.BlockSpec(vectors.shape, lambda i: (0, 0)),
+        rows, rows, rows, chances, rows, rows,
+    ]
+
+
+def back_scratch(width):
+    return [pltpu.VMEM((TILE, width), BF16)] * 4 + [pltpu.VMEM((4, width, width), F32)]
+
+
+def back_two(x, incoming, weight_stack, vectors, saved, d_up, d_down):
+    full = x.shape
+    frames, patches, width = full
+    half = width // 2
+    spots = TILE // frames
+    at = pl.BlockSpec((frames, spots, width), lambda i: (0, i, 0))
+    anywhere = pl.BlockSpec(memory_space=pl.ANY)
+    vmem = pl.BlockSpec(memory_space=pltpu.VMEM)
+    return pl.pallas_call(
+        back_two_kernel,
+        grid=(patches // spots,),
+        in_specs=back_specs(full, vectors, at, lambda i: i, 1) + [anywhere] * 2,
+        out_specs=[at, vmem, vmem, vmem, vmem],
+        out_shape=[
+            jax.ShapeDtypeStruct(full, BF16),
+            jax.ShapeDtypeStruct((2, 2, 2, half, width), BF16),
+            jax.ShapeDtypeStruct((8, width), F32),
+            jax.ShapeDtypeStruct((half, width), BF16),
+            jax.ShapeDtypeStruct((half, width), BF16),
+        ],
+        scratch_shapes=back_scratch(width)
+        + split_scratch(half, width)
+        + split_scratch(half, width),
+        compiler_params=pltpu.CompilerParams(
+            vmem_limit_bytes=VMEM_LIMIT, collective_id=3, has_side_effects=True
+        ),
+        name="back_two",
+    )(
+        x, incoming, weight_stack, vectors, *saved,
+        d_up.reshape(2, 2, 2, half, width), d_down.reshape(2, 2, 2, half, width),
+    )
+
+
+def back_one_kernel(
+    x_ref, d_ref, w_ref, vec_ref, q_ref, k_ref, v_ref, p_ref, o_ref, r_ref,
+    two_ref, up_ref, down_ref, y_ref, mixed_in,
+    one_ref, dvec_ref, two_out, early_ref, dx_out, mixed_ref, late_ref,
+    dq_ref, dk_ref, dv_ref, do_ref, acc_ref, dx_all, dx_sems, late_sem, near, away, core_sems, *sums,
+):
+    step = pl.program_id(0)
+    steps = pl.num_programs(0)
+    side, depth, line, core = places()
+    depths = lax.axis_size("clip")
+    mid = dx_all.shape[0] // 2
+    per_tile = TILE // BLOCK
+    two = line_sum(False, two_ref, *sums[:LINE])
+    up_parts = sums[LINE + 1]
+    down_parts = sums[LINE + DEPTH + 1]
+    up = depth_sum(2, up_ref, *sums[LINE : LINE + DEPTH])
+    down = depth_sum(3, down_ref, *sums[LINE + DEPTH :])
+    rows = one_ref.shape[2]
+    cores = [
+        remote(away.at[y, x], near.at[y, x], core_sems.at[0, y, x], core_sems.at[1, y, x], other_core())
+        for y in range(2)
+        for x in range(2)
+    ]
+
+    quarter = mid // 2
+    y_move = remote(
+        y_ref.at[pl.ds(mid + quarter, quarter)], mixed_ref.at[pl.ds(quarter, quarter)],
+        dx_sems.at[0, 1], dx_sems.at[1, 1], other_side(),
+    )
+    late = pltpu.make_async_copy(dx_all.at[pl.ds(mid + per_tile, per_tile)], late_ref, late_sem)
+
+    def dx_move(part):
+        return remote(
+            dx_all.at[pl.ds(mid + part * per_tile, per_tile)],
+            dx_out.at[side, pl.ds(part * per_tile, per_tile)],
+            dx_sems.at[0, part], dx_sems.at[1, part], other_side(),
+        )
+
+    def dx_own(part):
+        return pltpu.make_async_copy(
+            dx_all.at[pl.ds(part * per_tile, per_tile)],
+            dx_out.at[side, pl.ds(part * per_tile, per_tile)],
+            dx_sems.at[2, part],
+        )
+
+    @pl.when(step == 0)
+    def _():
+        greet(
+            [other_core(), other_side(), other_line()]
+            + [other_depth(distance) for distance in range(1, depths)]
+        )
+        two[0]()
+        y_move.start()
+        up[0]()
+        down[0]()
+
+    @pl.when(step == 1)
+    def _():
+        dx_move(0).start()
+        two[1]()
+
+    @pl.when(step == 2)
+    def _():
+        late.start()
+
+    @pl.when(step == 3)
+    def _():
+        dx_own(0).start()
+        down[1]()
+
+    def between():
+        @pl.when(step == 2)
+        def _():
+            up[1]()
+            two[2]()
+
+    def after():
+        @pl.when(step == steps - 1)
+        def _():
+            for y in range(2):
+                for x in range(2):
+                    place = pl.ds(x * rows, rows)
+                    away[y, x] = acc_ref[2 * y + 1 - core, place, :].astype(BF16)
+                    cores[2 * y + x].start()
+            for y in range(2):
+                for x in range(2):
+                    place = pl.ds(x * rows, rows)
+                    one_ref[y, x] = acc_ref[2 * y + core, place, :].astype(BF16)
+
+    result = attend_back_tile(
+        False, step, x_ref, d_ref, w_ref, vec_ref, q_ref, k_ref, v_ref, p_ref, o_ref, r_ref,
+        dvec_ref, dq_ref, dk_ref, dv_ref, do_ref, acc_ref, between, after,
+    )
+    tile = lax.rem(step + steps // 2, steps)
+    place = pl.ds(pl.multiple_of(tile * per_tile, per_tile), per_tile)
+    dx_all[place] = result.astype(BF16).reshape(per_tile, BLOCK, dx_all.shape[2])
+
+    @pl.when(step == steps - 1)
+    def _():
+        dx_own(1).start()
+        up[2]()
+        down[2]()
+
+        @pl.when(depth == 3)
+        def _():
+            early_ref[...] = down_parts[...]
+
+        @pl.when(depth != 3)
+        def _():
+            early_ref[...] = up_parts[...]
+
+        two[3](two_out)
+        two[4]()
+        up[3]()
+        down[3]()
+        for y in range(2):
+            for x in range(2):
+                cores[2 * y + x].wait()
+                add_rows(one_ref.at[y, x], near.at[y, x], rows)
+        dx_move(0).wait()
+        y_move.wait()
+        late.wait()
+        for part in range(2):
+            dx_own(part).wait()
+
+
+def back_one(x, incoming, weight_stack, vectors, saved, d_two, part_up, part_down, mixed, mixed_part):
+    full = x.shape
+    frames, patches, width = full
+    half = width // 2
+    per_tile = TILE // patches
+    steps = frames // per_tile
+    turned = lambda i: lax.rem(i + steps // 2, steps)
+    at = pl.BlockSpec((TILE, width), lambda i: (turned(i), 0))
+    anywhere = pl.BlockSpec(memory_space=pl.ANY)
+    vmem = pl.BlockSpec(memory_space=pltpu.VMEM)
+    dma = pltpu.SemaphoreType.DMA
+    return pl.pallas_call(
+        back_one_kernel,
+        grid=(steps,),
+        in_specs=back_specs(full, vectors, at, turned, 0) + [anywhere, vmem, vmem, anywhere, anywhere],
+        out_specs=[vmem] * 4 + [anywhere] * 3,
+        out_shape=[
+            jax.ShapeDtypeStruct((2, 2, half, width), BF16),
+            jax.ShapeDtypeStruct((8, width), F32),
+            jax.ShapeDtypeStruct((half, width), BF16),
+            jax.ShapeDtypeStruct((half, width), BF16),
+            jax.ShapeDtypeStruct((2, frames // 2, patches, width), BF16),
+            jax.ShapeDtypeStruct((frames // 2, patches, width), BF16),
+            jax.ShapeDtypeStruct((per_tile, patches, width), BF16),
+        ],
+        input_output_aliases={14: 5},
+        scratch_shapes=back_scratch(width)
+        + [pltpu.VMEM(full, BF16), dma((3, 2)), dma]
+        + [pltpu.VMEM((2, 2, half, width), BF16)] * 2
+        + [dma((2, 2, 2))]
+        + line_scratch(half, width)
+        + depth_scratch(half, width) * 2,
+        compiler_params=pltpu.CompilerParams(
+            vmem_limit_bytes=VMEM_LIMIT, collective_id=4, has_side_effects=True
+        ),
+        name="back_one",
+    )(
+        x.reshape(frames * patches, width), incoming.reshape(frames * patches, width), weight_stack, vectors,
+        *saved, d_two, part_up, part_down, mixed, mixed_part,
+    )
+
+
+PARTS = 2
+
+
+def update_kernel(
+    one_ref, late_ref, two_ref, early_ref, v1_ref, v2_ref, v3_ref, vec_ref, m_ref,
+    nm_ref, full, vsum_ref, vnew_ref, dx_ref,
+    total, vgot, vsent, v_send, v_got, m_send, m_got, x_send, x_got, *sums,
+):
+    side, depth, line, core = places()
+    depths = lax.axis_size("clip")
+    half, width = nm_ref.shape
+    share = half // PARTS
+    at = SPLIT * PARTS
+    one = [
+        split_sum(False, one_ref, *sums[SPLIT * p : SPLIT * (p + 1)], part=p)
+        for p in range(PARTS)
+    ]
+    one_z = [
+        depth_sum(0, total.at[p], *sums[at + DEPTH * p : at + DEPTH * (p + 1)]) for p in range(PARTS)
+    ]
+    one_parts = [sums[at + DEPTH * p + 1] for p in range(PARTS)]
+    two_z = depth_sum(1, two_ref, *sums[at + DEPTH * PARTS :])
+    two_parts = sums[at + DEPTH * PARTS + 1]
+    for p in range(PARTS):
+        one[p][0]()
+    greet(
+        [other_core(), other_side(), other_line()]
+        + [other_depth(step) for step in range(1, depths)]
+    )
+    vsent[0] = jnp.zeros(vsent.shape[1:], F32)
+    order = (
+        (v1_ref, 0), (v2_ref, 0), (v3_ref, 0), (v1_ref, 1), (v2_ref, 1), (v3_ref, 1),
+        (v1_ref, 2), (v1_ref, 3), (v1_ref, 4), (v2_ref, 2), (v2_ref, 3), (v2_ref, 4),
+        (v3_ref, 2), (v3_ref, 3), (v3_ref, 4), (v3_ref, 5), (v3_ref, 6),
+    )
+    for row, (ref, place) in enumerate(order):
+        vsent[0, row : row + 1] = ref[place : place + 1]
+    vcopies = []
+
+    def exchange_vec(step):
+        if step >= 1:
+            vcopies[step - 1].wait_recv()
+            if step < 3:
+                vsent[step] = vsent[step - 1] + vgot[step - 1]
+        if step < 3:
+            device = (other_core, other_side, other_line)[step]()
+            vcopies.append(remote(vsent.at[step], vgot.at[step], v_send.at[step], v_got.at[step], device))
+            vcopies[-1].start()
+        else:
+            vgot[3 + depth] = vsent[step - 1] + vgot[step - 1]
+            for distance in range(1, depths):
+                vcopies.append(
+                    remote(
+                        vgot.at[3 + depth], vgot.at[3 + depth],
+                        v_send.at[2 + distance], v_got.at[2 + distance], other_depth(distance),
+                    )
+                )
+                vcopies[-1].start()
+
+    def swap(p, of):
+        rows = full.at[pl.ds(pl.multiple_of(of * half + p * share, 16), share)]
+        return remote(rows, rows, m_send.at[p], m_got.at[p], other_side())
+
+    def step_rows(p, grad_of):
+        def one_part(index, carry):
+            rows = pl.ds(pl.multiple_of(index * 48, 48), 48)
+            place = pl.ds(pl.multiple_of(p * share + index * 48, 48), 48)
+            moment = DECAY * m_ref[place, :] + grad_of(rows, place).astype(F32)
+            nm_ref[place, :] = moment
+            full[pl.ds(pl.multiple_of(side * half + p * share + index * 48, 16), 48), :] = moment.astype(BF16)
+            return carry
+
+        lax.fori_loop(0, share // 48, one_part, 0)
+
+    def renew(p):
+        @pl.when(depth == 0)
+        def _():
+            step_rows(p, lambda rows, place: one_parts[p][rows, :])
+
+        @pl.when(depth == 1)
+        def _():
+            step_rows(p, lambda rows, place: two_parts[place, :])
+
+        @pl.when(depth >= 2)
+        def _():
+            step_rows(p, lambda rows, place: early_ref[place, :])
+
+        swap(p, side).start()
+
+    exchange_vec(0)
+    for p in range(PARTS):
+        one[p][1]()
+    two_z[0]()
+    exchange_vec(1)
+    for p in range(PARTS):
+        one[p][2]()
+    dx_move = remote(late_ref, dx_ref, x_send, x_got, other_side())
+    dx_move.start()
+    exchange_vec(2)
+    two_z[1]()
+    for p in range(PARTS):
+        one[p][3](total.at[p])
+        one_z[p][0]()
+    exchange_vec(3)
+    for p in range(PARTS):
+        one_z[p][1]()
+    two_z[2]()
+    for p in range(PARTS):
+        one_z[p][2]()
+        renew(p)
+    for distance in range(1, depths):
+        remote(
+            vgot.at[3], vgot.at[3 + lax.rem(depth + depths - distance, depths)],
+            v_send.at[2 + distance], v_got.at[2 + distance], other_depth(distance),
+        ).wait_recv()
+    vsum = vgot[3]
+    for z in range(1, depths):
+        vsum = vsum + vgot[3 + z]
+    rows = vsum_ref.shape[0]
+    vsum_ref[...] = vsum[:rows]
+    vnew_ref[...] = vec_ref[...] - VECTOR_RATE * (65536.0 ** (-0.5)) * vsum[:rows]
+    for p in range(PARTS):
+        swap(p, 1 - side).wait_recv()
+        one[p][4]()
+        one_z[p][3]()
+    two_z[3]()
+    dx_move.wait()
+    for copy in vcopies:
+        copy.wait_send()
+    for p in range(PARTS):
+        swap(p, side).wait_send()
+
+
+def update(d_one, late, part_two, early, vec_one, vec_two, vec_three, vectors, momentum):
+    half, width = momentum.shape
+    depths = lax.axis_size("clip")
+    dma = pltpu.SemaphoreType.DMA
+    anywhere = pl.BlockSpec(memory_space=pl.ANY)
+    vmem = pl.BlockSpec(memory_space=pltpu.VMEM)
+    return pl.pallas_call(
+        update_kernel,
+        in_specs=[anywhere] * 2 + [vmem] * 7,
+        out_specs=[vmem] * 4 + [anywhere],
+        out_shape=[
+            jax.ShapeDtypeStruct((half, width), F32),
+            jax.ShapeDtypeStruct((width, width), BF16),
+            jax.ShapeDtypeStruct(vectors.shape, F32),
+            jax.ShapeDtypeStruct(vectors.shape, F32),
+            jax.ShapeDtypeStruct(late.shape, BF16),
+        ],
+        scratch_shapes=[
+            pltpu.VMEM((PARTS, half // PARTS, width), BF16),
+            pltpu.VMEM((3 + depths, 24, width), F32),
+            pltpu.VMEM((3, 24, width), F32),
+            dma((2 + depths,)), dma((2 + depths,)),
+            dma((PARTS,)), dma((PARTS,)),
+            dma, dma,
+        ]
+        + split_scratch(half // PARTS, width, False) * PARTS
+        + depth_scratch(half // PARTS, width) * PARTS
+        + depth_scratch(half, width),
+        compiler_params=pltpu.CompilerParams(
+            vmem_limit_bytes=VMEM_LIMIT, collective_id=1, has_side_effects=True
+        ),
+        name="update",
+    )(d_one.reshape(2, 2, PARTS, half // PARTS, width), late, part_two, early, vec_one, vec_two, vec_three, vectors, momentum)
+
+
+def finish_kernel(
+    full, w_ref, nm_in, vsum_in, vnew_in, y_in, mixed_in, dx_in, late_in,
+    nw_ref, low_ref, nm_ref, vsum_ref, vnew_ref, mixed_ref, dx_ref,
+    x_acc, a_low, p_low, y_all, dx_all, sems,
+):
+    side, depth, line, core = places()
+    half = w_ref.shape[0]
+    mid = mixed_in.shape[0]
+    loads = [
+        pltpu.make_async_copy(y_in.at[pl.ds(0, mid)], y_all.at[side], sems.at[0]),
+        pltpu.make_async_copy(mixed_in, y_all.at[1 - side], sems.at[1]),
+        pltpu.make_async_copy(dx_in.at[side], dx_all.at[side], sems.at[2]),
+        pltpu.make_async_copy(
+            dx_in.at[1 - side, pl.ds(0, mid // 2)], dx_all.at[1 - side, pl.ds(0, mid // 2)], sems.at[5]
+        ),
+        pltpu.make_async_copy(late_in, dx_all.at[1 - side, pl.ds(mid // 2, mid // 2)], sems.at[6]),
+    ]
+    stores = [
+        pltpu.make_async_copy(y_all, mixed_ref, sems.at[3]),
+        pltpu.make_async_copy(dx_all, dx_ref, sems.at[4]),
+    ]
+    for copy in loads:
+        copy.start()
+    nm_ref[...] = nm_in[...]
+    vsum_ref[...] = vsum_in[...]
+    vnew_ref[...] = vnew_in[...]
+    mine = pl.ds(pl.multiple_of(side * half, half), half)
+    moment = full[...].astype(F32)
+    squares = jnp.sum(jnp.sum(moment * moment, 0, keepdims=True), 1, keepdims=True)
+    x_acc[...] = moment * (1.0 / (jnp.sqrt(squares) + 1e-07))
+    for sweep in range(NS_STEPS):
+        low = x_acc[...].astype(BF16)
+        gram = dot(low, low, 1, 1)
+        a_low[...] = gram.astype(BF16)
+        if sweep < NS_STEPS - 1:
+            p_low[...] = (NS_B * gram + NS_C * dot(a_low[...], a_low[...])).astype(BF16)
+            x_acc[...] = NS_A * x_acc[...] + dot(p_low[...], low)
+            for copy in loads:
+                copy.wait()
+            for copy in stores:
+                copy.start()
+        else:
+            part = a_low[mine, :]
+            power = (NS_B * part.astype(F32) + NS_C * dot(part, a_low[...])).astype(BF16)
+            block = 4 * depth + 2 * line + core
+            factor = jnp.where(block == 3, 4.0, jnp.where(block == 7, 2.0, jnp.where(block >= 12, 0.5, 1.0)))
+            result = NS_A * x_acc[mine, :] + dot(power, low)
+            renewed = w_ref[...] - MUON_RATE * factor * result
+            nw_ref[...] = renewed
+            low_ref[...] = renewed.astype(BF16)
+    for copy in stores:
+        copy.wait()
+
+
+def finish(full, weights, new_momentum, vector_sum, new_vectors, y, mixed, dx, late):
+    half, width = weights.shape
+    anywhere = pl.BlockSpec(memory_space=pl.ANY)
+    vmem = pl.BlockSpec(memory_space=pltpu.VMEM)
+    return pl.pallas_call(
+        finish_kernel,
+        in_specs=[vmem] * 5 + [anywhere] * 4,
+        out_specs=[vmem] * 5 + [anywhere] * 2,
+        out_shape=[
+            jax.ShapeDtypeStruct((half, width), F32),
+            jax.ShapeDtypeStruct((half, width), BF16),
+            jax.ShapeDtypeStruct((half, width), F32),
+            jax.ShapeDtypeStruct(vector_sum.shape, F32),
+            jax.ShapeDtypeStruct(vector_sum.shape, F32),
+            jax.ShapeDtypeStruct(dx.shape, BF16),
+            jax.ShapeDtypeStruct(dx.shape, BF16),
+        ],
+        scratch_shapes=[
+            pltpu.VMEM((width, width), F32),
+            pltpu.VMEM((width, width), BF16),
+            pltpu.VMEM((width, width), BF16),
+            pltpu.VMEM(dx.shape, BF16),
+            pltpu.VMEM(dx.shape, BF16),
+            pltpu.SemaphoreType.DMA((7,)),
+        ],
+        compiler_params=pltpu.CompilerParams(vmem_limit_bytes=VMEM_LIMIT),
+        name="finish",
+    )(full, weights, new_momentum, vector_sum, new_vectors, y, mixed, dx, late)
+
+
+def attend_tile(temporal, start, weight, vec_ref, q_ref, k_ref, v_ref, p_ref, o_ref, r_ref):
+    first = 1 if temporal else 0
+    bias = 9 if temporal else 6
+    normal, inverse = row_stats(start)
+    normed = (normal * vec_ref[first : first + 1] + vec_ref[first + 3 : first + 4]).astype(BF16)
+    q_ref[...] = (dot(normed, weight(0)) + vec_ref[bias : bias + 1]).astype(BF16)
+    k_ref[...] = dot(normed, weight(1)).astype(BF16)
+    v_ref[...] = (dot(normed, weight(2)) + vec_ref[bias + 1 : bias + 2]).astype(BF16)
+    masks = half_masks()
+    mask = place_mask() if temporal else None
+    sums = head_sums()
+
+    def one_block(block, carry):
+        rows = pl.ds(pl.multiple_of(block * BLOCK, BLOCK), BLOCK)
+        pairs = lane_pairs()
+        scores = [dot(q_ref[rows, lanes], stacked(k_ref[rows, lanes], masks), 1, 1) for lanes in pairs]
+        powers = [powers_of(score, mask) for score in scores]
+        mixes = []
+        for pair, lanes in enumerate(pairs):
+            p_ref[block, pair] = powers[pair]
+            values = jnp.concatenate([stacked(v_ref[rows, lanes], masks), sums], 1)
+            mixes.append(dot(powers[pair], values))
+        for mix, lanes in zip(mixes, pairs):
+            inverse_sum = 1.0 / mix[:, BLOCK:]
+            r_ref[rows, lanes] = inverse_sum
+            o_ref[rows, lanes] = (mix[:, :BLOCK] * inverse_sum).astype(BF16)
+        return carry
+
+    lax.fori_loop(0, TILE // BLOCK, one_block, 0)
+    return dot(o_ref[...], weight(3)) + vec_ref[bias + 2 : bias + 3]
+
+
+PIECES = 4
+ARRIVALS = {
+    (2, 2): (1, 1),
+    (2, 3): (0, 1),
+    (1, 2): (0, 2),
+    (1, 3): (2, 3),
+    (3, 2): (5, 8),
+    (0, 2): (5, 8),
+    (0, 3): (8, 8),
+}
+SECOND = {0: (0, 2), 2: (-1, 0), 3: (1, 2)}
+
+
+def front_kernel(
+    t_ref, g_ref, w_ref, vec_ref,
+    w_out, x_out, g_out,
+    q1_ref, k1_ref, v1_ref, p1_ref, o1_ref, r1_ref, y1_ref,
+    q2_ref, k2_ref, v2_ref, p2_ref, o2_ref, r2_ref, y2_ref,
+    w_all, x_all, x1_all,
+    near_send, near_got, up_send, up_got, sx_send, sx_got, sy_send, sy_got, di_send, di_got,
+    px_send, px_got, pz_send, pz_got, py_send, py_got, pc_send, pc_got,
+    su_send, su_got, sl_send, sl_got,
+    tok_send, tok_got, load_sem,
+):
+    step = pl.program_id(0)
+    side, depth, line, core = places()
+    depths = lax.axis_size("clip")
+    last = depths - 1
+    half, width = w_ref.shape
+    frames = x_all.shape[0]
+    mid = frames // 2
+    per_tile = TILE // x_all.shape[1]
+    halves = pl.num_programs(0) // 2
+    left = slice(0, width // 2)
+    right = slice(width // 2, width)
+
+    def piece(g, h):
+        return w_all.at[g, line, core, side if h == 0 else 1 - side]
+
+    def move_up(g, h):
+        return remote(piece(g, h), piece(g, h), pz_send.at[g, h, 0], pz_got.at[g, h], {"clip": depth + 1})
+
+    def move_down(g, h):
+        return remote(piece(g, h), piece(g, h), pz_send.at[g, h, 1], pz_got.at[g, h], {"clip": depth - 1})
+
+    def move_line(g, h):
+        return remote(piece(g, h), piece(g, h), py_send.at[g, h], py_got.at[g, h], other_line())
+
+    def from_line(g, h):
+        place = w_all.at[g, 1 - line, core, side if h == 0 else 1 - side]
+        return remote(place, place, py_send.at[g, h], py_got.at[g, h], other_line())
+
+    core_parts = [(line, None), (1 - line, 0), (1 - line, 1)]
+
+    def second_core(part, received=False):
+        line_at, h = core_parts[part]
+        place = w_all.at[1, line_at, 1 - core if received else core]
+        if h is not None:
+            place = place.at[side if h == 0 else 1 - side]
+        return remote(place, place, pc_send.at[part], pc_got.at[part], other_core())
+
+    own_side = remote(piece(depth, 0), piece(depth, 0), px_send, px_got, other_side())
+    from_side = remote(piece(depth, 1), piece(depth, 1), px_send, px_got, other_side())
+
+    def token_move(part):
+        return remote(
+            x1_all.at[pl.ds(mid + part * per_tile, per_tile)],
+            x_all.at[pl.ds(mid + part * per_tile, per_tile)],
+            tok_send.at[part], tok_got.at[part], other_side(),
+        )
+
+    token_parts = mid // per_tile
+
+    def grad_move(part):
+        place = (pl.ds(0, mid // 2), pl.ds(mid // 2, mid // 4))[part]
+        return remote(
+            g_ref.at[1 - side, place], g_out.at[place],
+            tok_send.at[token_parts + part], tok_got.at[token_parts + part], other_side(),
+        )
+
+    token_own = pltpu.make_async_copy(t_ref.at[side], x_all.at[pl.ds(0, mid)], load_sem.at[0])
+    token_other = pltpu.make_async_copy(t_ref.at[1 - side], x1_all.at[pl.ds(mid, mid)], load_sem.at[7])
+    outs = [
+        pltpu.make_async_copy(place, target, load_sem.at[1 + k])
+        for k, (place, target) in enumerate(
+            [(w_all.at[g], w_out.at[g]) for g in range(2)]
+            + [(w_all.at[g, line, core], w_out.at[g, line, core]) for g in range(2, depths)]
+            + [(w_all.at[2, 1 - line, core, side], w_out.at[2, 1 - line, core, side])]
+        )
+    ]
+    keep = pltpu.make_async_copy(x_all, x_out, load_sem.at[6])
+
+    def arrive(g, h, at):
+        @pl.when(depth == at)
+        def _():
+            if at != g:
+                move_up(g, h).wait_recv()
+            if g <= at < last:
+                move_up(g, h).start()
+            if 0 < at < g:
+                move_down(g, h).start()
+            if (g, h) == (2, 0):
+                move_line(g, h).start()
+
+    def second(e, line_at):
+        rows = pl.ds((e % 2) * (half // 2), half // 2)
+        return w_all.at[1, line_at, core, side if e < 2 else 1 - side, rows]
+
+    def second_up(e):
+        return same(second(e, line), su_send.at[e], su_got.at[e], {"clip": depth + 1})
+
+    def second_line(e, received=False):
+        return same(second(e, 1 - line if received else line), sl_send.at[e], sl_got.at[e], other_line())
+
+    def arrivals(slot):
+        for at, slots in SECOND.items():
+            for h in range(2):
+                if slots[h] == slot:
+
+                    @pl.when(depth == at)
+                    def _():
+                        if at == 0:
+                            move_up(1, h).wait_recv()
+                        for e in (2 * h, 2 * h + 1):
+                            if at > 0:
+                                second_up(e).wait_recv()
+                            if 0 < at < last:
+                                second_up(e).start()
+                            second_line(e).start()
+
+        for (at, g), slots in ARRIVALS.items():
+            for h in range(2):
+                if slots[h] == slot:
+                    arrive(g, h, at)
+
+    def first(k, line_at, side_at, columns=slice(None)):
+        return w_all.at[0, line_at, core, side_at, pl.ds(k * (half // PIECES), half // PIECES), columns]
+
+    def same(place, send, got, device):
+        return remote(place, place, send, got, device)
+
+    def first_up(k):
+        return same(first(k, line, side), up_send.at[k], up_got.at[k], {"clip": depth + 1})
+
+    def first_side(k, received=False):
+        return same(first(k, line, 1 - side if received else side), sx_send.at[k], sx_got.at[k], other_side())
+
+    def first_line(k, received=False):
+        return same(first(k, 1 - line if received else line, side), sy_send.at[k], sy_got.at[k], other_line())
+
+    def first_cross(k, way, received=False):
+        if received:
+            place = first(k, 1 - line, 1 - side, (left, right)[way])
+        elif way == 0:
+            place = first(k, 1 - line, side, left)
+        else:
+            place = first(k, line, 1 - side, right)
+        return same(place, di_send.at[k, way], di_got.at[k, way], (other_side, other_line)[way]())
+
+    spots = [(line, side), (1 - line, side), (line, 1 - side), (1 - line, 1 - side)]
+
+    def first_core(k, spot, received=False):
+        line_at, side_at = spots[spot]
+        place = w_all.at[
+            0, line_at, 1 - core if received else core, side_at, pl.ds(k * (half // PIECES), half // PIECES)
+        ]
+        return same(place, near_send.at[k, spot], near_got.at[k, spot], other_core())
+
+    @pl.when(step == 0)
+    def _():
+        greet(
+            [other_core(), other_side(), other_line()]
+            + [other_depth(distance) for distance in range(1, depths)]
+        )
+        token_own.start()
+        token_other.start()
+        w_all[depth, line, core, side] = w_ref[...].astype(BF16)
+
+        @pl.when(depth > 0)
+        def _():
+            own_side.start()
+
+        @pl.when(depth > 0)
+        def _():
+            move_down(depth, 0).start()
+
+        for k in range(PIECES):
+
+            @pl.when(depth > 0)
+            def _():
+                first_up(k).wait_recv()
+
+            @pl.when(depth < last)
+            def _():
+                first_up(k).start()
+
+            first_side(k).start()
+            first_line(k).start()
+            first_core(k, 0).start()
+
+        @pl.when(depth == 1)
+        def _():
+            for e in (0, 1):
+                second_up(e).start()
+
+        @pl.when(depth > 0)
+        def _():
+            from_side.wait_recv()
+            move_down(depth, 1).start()
+
+        @pl.when(depth == 1)
+        def _():
+            for e in (2, 3):
+                second_up(e).start()
+            for e in range(4):
+                second_line(e).start()
+
+        for k in range(PIECES):
+            first_line(k, True).wait_recv()
+            first_cross(k, 0).start()
+            first_core(k, 1).start()
+            first_side(k, True).wait_recv()
+            first_cross(k, 1).start()
+            first_core(k, 2).start()
+        arrivals(-1)
+        token_other.wait()
+        token_move(0).start()
+        for k in range(PIECES):
+            first_cross(k, 0, True).wait_recv()
+            first_cross(k, 1, True).wait_recv()
+            first_core(k, 3).start()
+        for k in range(PIECES):
+            for spot in range(4):
+                first_core(k, spot, True).wait_recv()
+        token_move(1).start()
+        arrivals(0)
+        token_own.wait()
+
+    for slot in range(1, 8):
+
+        @pl.when(step == slot)
+        def _():
+            if slot == 1:
+                outs[0].start()
+            if slot == 2:
+                token_move(0).wait()
+            if slot == 3:
+                token_move(1).wait()
+                grad_move(0).start()
+                keep.start()
+            arrivals(slot)
+            if slot == 2:
+                second_core(0).start()
+            if slot == 3:
+                for e in range(2):
+                    second_line(e, True).wait_recv()
+                second_core(1).start()
+            if slot == 5:
+                grad_move(1).start()
+            if slot == 4:
+                for e in range(2, 4):
+                    second_line(e, True).wait_recv()
+                second_core(2).start()
+                for part in range(3):
+                    second_core(part, True).wait_recv()
+                outs[1].start()
+
+    @pl.when(step < halves)
+    def _():
+        place = pl.ds(pl.multiple_of(step * per_tile, per_tile), per_tile)
+        start = x_all[place].astype(F32).reshape(TILE, width)
+        branch = attend_tile(
+            False, start, lambda b: w_all[0, b // 2, b % 2].reshape(width, width), vec_ref,
+            q1_ref, k1_ref, v1_ref, p1_ref, o1_ref, r1_ref,
+        )
+        start = x_all[place].astype(F32).reshape(TILE, width)
+        result = (start + branch).astype(BF16).reshape(per_tile, BLOCK, width)
+        y1_ref[...] = result
+        x1_all[place] = result
+
+    @pl.when(step >= halves)
+    def _():
+        spots = TILE // frames
+        place = pl.ds(pl.multiple_of((step - halves) * spots, spots), spots)
+        tile_ref = x1_all.at[:, place, :]
+        branch = attend_tile(
+            True, load_rows(tile_ref, True), lambda b: w_all[1, b // 2, b % 2].reshape(width, width), vec_ref,
+            q2_ref, k2_ref, v2_ref, p2_ref, o2_ref, r2_ref,
+        )
+        store_rows(y2_ref, load_rows(tile_ref, True) + branch, True)
+
+    @pl.when(step == 2 * halves - 1)
+    def _():
+        arrivals(8)
+        from_line(2, 0).wait_recv()
+        for copy in outs[2:]:
+            copy.start()
+        for part in range(2):
+            grad_move(part).wait()
+        keep.wait()
+        for copy in outs:
+            copy.wait()
+
+        @pl.when(depth > 0)
+        def _():
+            own_side.wait_send()
+
+        for k in range(PIECES):
+
+            @pl.when(depth < last)
+            def _():
+                first_up(k).wait_send()
+
+            first_side(k).wait_send()
+            first_line(k).wait_send()
+            first_cross(k, 0).wait_send()
+            first_cross(k, 1).wait_send()
+            for spot in range(4):
+                first_core(k, spot).wait_send()
+        for h in range(2):
+
+            @pl.when(depth == 2)
+            def _():
+                move_up(2, h).wait_send()
+
+            for g in range(1, depths):
+
+                @pl.when((depth > 0) & (depth <= g))
+                def _():
+                    move_down(g, h).wait_send()
+
+        for e in range(4):
+
+            @pl.when((depth > 0) & (depth < last))
+            def _():
+                second_up(e).wait_send()
+
+            second_line(e).wait_send()
+        move_line(2, 0).wait_send()
+        for part in range(3):
+            second_core(part).wait_send()
+
+
+def front(tokens, cotangent, weights, vectors):
+    _, mid, patches, width = tokens.shape
+    half = weights.shape[0]
+    frames = 2 * mid
+    count = frames * patches
+    halves = count // TILE
+    depths = lax.axis_size("clip")
+    dma = pltpu.SemaphoreType.DMA
+    anywhere = pl.BlockSpec(memory_space=pl.ANY)
+    one = lambda i: jnp.minimum(i, halves - 1)
+    two = lambda i: jnp.maximum(i - halves, 0)
+
+    def saved(at):
+        rows = pl.BlockSpec((TILE, width), lambda i: (at(i), 0))
+        chances = pl.BlockSpec((TILE // BLOCK, PAIRS, BLOCK, 2 * BLOCK), lambda i: (at(i), 0, 0, 0))
+        return [rows, rows, rows, chances, rows, rows]
+
+    rows_shape = jax.ShapeDtypeStruct((count, width), BF16)
+    saved_shape = [
+        rows_shape,
+        rows_shape,
+        rows_shape,
+        jax.ShapeDtypeStruct((count // BLOCK, PAIRS, BLOCK, 2 * BLOCK), BF16),
+        rows_shape,
+        jax.ShapeDtypeStruct((count, width), F32),
+    ]
+    full = jax.ShapeDtypeStruct((frames, patches, width), BF16)
+    stack = (depths, 2, 2, 2, half, width)
+    outs = pl.pallas_call(
+        front_kernel,
+        grid=(2 * halves,),
+        in_specs=[
+            anywhere,
+            anywhere,
+            pl.BlockSpec((half, width), lambda i: (0, 0), pipeline_mode=pl.Buffered(1)),
+            pl.BlockSpec(vectors.shape, lambda i: (0, 0)),
+        ],
+        out_specs=[anywhere] * 3
+        + saved(one)
+        + [pl.BlockSpec((TILE // patches, patches, width), lambda i: (one(i), 0, 0))]
+        + saved(two)
+        + [pl.BlockSpec((frames, TILE // frames, width), lambda i: (0, two(i), 0))],
+        out_shape=[
+            jax.ShapeDtypeStruct(stack, BF16),
+            full,
+            jax.ShapeDtypeStruct((mid, patches, width), BF16),
+        ]
+        + saved_shape
+        + [full]
+        + saved_shape
+        + [full],
+        scratch_shapes=[
+            pltpu.VMEM(stack, BF16),
+            pltpu.VMEM((frames, patches, width), BF16),
+            pltpu.VMEM((frames, patches, width), BF16),
+            dma((PIECES, 4)), dma((PIECES, 4)),
+            dma((PIECES,)), dma((PIECES,)),
+            dma((PIECES,)), dma((PIECES,)),
+            dma((PIECES,)), dma((PIECES,)),
+            dma((PIECES, 2)), dma((PIECES, 2)),
+            dma, dma,
+            dma((depths, 2, depths)), dma((depths, 2)),
+            dma((depths, 2)), dma((depths, 2)),
+            dma((depths,)), dma((depths,)),
+            dma((4,)), dma((4,)),
+            dma((4,)), dma((4,)),
+            dma((mid * patches // TILE + 2,)), dma((mid * patches // TILE + 2,)),
+            dma((8,)),
+        ],
+        compiler_params=pltpu.CompilerParams(
+            vmem_limit_bytes=VMEM_LIMIT, collective_id=2, has_side_effects=True
+        ),
+        name="front",
+    )(tokens, cotangent, weights, vectors)
+    stacked_weights, x0, gy = outs[:3]
+    return stacked_weights, x0, gy, outs[3:9], outs[9], outs[10:16], outs[16]
+
+
+def paired_body(tokens, cotangent, weights, momentum, vectors):
+    weight_stack, x0, grad_part, saved_one, x1, saved_two, x2 = front(
+        tokens[:, 0], cotangent[:, 0], weights[0], vectors
+    )
+    full = x0.shape
+    mixed, dx2, d_up, d_down, vec_three, mixed_part = feed(
+        x2.reshape(full[0] * full[1], full[2]), cotangent[:, 0], grad_part, weight_stack, vectors
+    )
+    mixed = mixed.reshape(full)
+    weight_stack = weight_stack.reshape(-1, full[2], full[2])
+    dx1, d_two, vec_two, part_up, part_down = back_two(
+        x1, dx2.reshape(full), weight_stack, vectors, saved_two, d_up, d_down
+    )
+    d_one, vec_one, part_two, early, grad_out, mixed_part, late = back_one(
+        x0, dx1, weight_stack, vectors, saved_one, d_two, part_up, part_down, mixed, mixed_part
+    )
+    new_momentum, moment, vector_sum, new_vectors, late = update(
+        d_one, late, part_two, early, vec_one, vec_two, vec_three, vectors, momentum[0]
+    )
+    new_weights, new_low, new_momentum, vector_sum, new_vectors, mixed_out, grad_out = finish(
+        moment, weights[0], new_momentum, vector_sum, new_vectors, mixed, mixed_part, grad_out, late
+    )
+    return (
+        mixed_out[:, None],
+        grad_out[:, None],
+        new_momentum[None],
+        new_weights[None],
+        new_low[None],
+        vector_sum,
+        new_vectors,
+    )
+
+
 def solution(mesh):
     in_specs = (
         P(None, ("clip", "fsdp"), "seq", None, None),
@@ -418,4 +2083,6 @@
         P(),
         P(),
     )
-    return jax.shard_map(body, mesh=mesh, in_specs=in_specs, out_specs=out_specs, check_vma=False)
+    paired = dict(mesh.shape) == {"clip": 4, "seq": 2, "fsdp": 4}
+    program = paired_body if paired else body
+    return jax.shard_map(program, mesh=mesh, in_specs=in_specs, out_specs=out_specs, check_vma=False)

time: 1420 us -> 400 us (0.28)
  matrix products: 501 us -> 0 us
  waiting for transfers between devices: 394 us -> 0 us
  Pallas kernels: 0 us -> 393 us
  local copies, waits for them, and re-layouts: 265 us -> 0 us
  other arithmetic: 153 us -> 0 us
  blocking collectives: 39.8 us -> 0 us
  starting transfers between devices: 35 us -> 0 us
  between operations: 17.3 us -> 0.96 us
    dot_general x90 -> x0, matrix products: 501 us -> none  [the longest x16 65.7 us: multiply_back(): jnp.einsum('...e,de->...d', grads, matrix, preferred_element_type=jnp.flo...]
    pallas_call x0 -> x6, Pallas kernels: none -> 393 us  [the longest x1 119 us: front(): pl.pallas_call(front_kernel, grid=(2 * halves,), in_specs=[anywhere, anyw...]
    reduce_scatter x2 -> x0, waiting for transfers between devices: 212 us -> none  [reduce_grads(): lax.psum_scatter(weight_grads.astype(jnp.bfloat16), ('clip', 'fsdp'), sca...]
    all_gather x3 -> x0, waiting for transfers between devices: 138 us -> none  [the longest x1 98.1 us: gather_weights(): return lax.all_gather(row_full, ('clip', 'fsdp'), axis=0, tiled=True)]
    convert_element_type x32 -> x0, local copies, waits for them, and re-layouts: 117 us -> none  [the longest x4 20.6 us: layer_pass(): flat_view(grad_query).astype(jnp.bfloat16)]
    convert_element_type x14 -> x0, other arithmetic: 101 us -> none  [the longest x1 62.4 us: layer_pass(): active_low = activated.astype(jnp.bfloat16)]
    another operation x50 -> x0, local copies, waits for them, and re-layouts: 79 us -> none  [the longest x16 39.4 us: layer_pass(): jnp.stack([d_query_one, d_key_one, d_value_one, d_out_one, d_query_two, d...]
    unnamed x346 -> x0, local copies, waits for them, and re-layouts: 60.9 us -> none
  transfers between devices with their start and end apart: 15 -> 0, of which waited for: 9 -> 0; matrix products, arithmetic and copies ran while one was open for 26% -> 0% of each run, Pallas kernels for 0% -> 0%
where the time goes in v1:
time: 400 us; the launch traced here: 394 us
  Pallas kernels  393 us (98%)
    pallas_call x1, Pallas kernels, front(): pl.pallas_call(front_kernel, grid=(2 * halves,), in_specs=[anywhere, anyw...  119 us
    pallas_call x1, Pallas kernels, feed(): pl.pallas_call(feed_kernel, grid=(chunks, steps), in_specs=[whole, pl.Blo...  87.6 us
    pallas_call x1, Pallas kernels, update(): pl.pallas_call(update_kernel, in_specs=[anywhere] * 2 + [vmem] * 7, out_s...  62.9 us
    pallas_call x1, Pallas kernels, back_one(): pl.pallas_call(back_one_kernel, grid=(steps,), in_specs=back_specs(full,...  58.3 us
    pallas_call x1, Pallas kernels, back_two(): pl.pallas_call(back_two_kernel, grid=(patches // spots,), in_specs=back_s...  55.2 us
    pallas_call x1, Pallas kernels, finish(): pl.pallas_call(finish_kernel, in_specs=[vmem] * 5 + [anywhere] * 4, out_s...  10.1 us

profile of v1, /device:TPU:0, one launch (start us, length us, event | category | flops | bytes accessed | tf_op | source)
XLA Modules:
  0.0 394.0 jit_solution(14837368552005834908)
XLA Ops:
  0.6 118.9 %front.1 = (bf16[4,2,2,2,384,768]{5,4,3,2,1,0:T(8,128)(2,1)}, bf16[16,128,768]{2,1,0:T(8,128)(2,1)}, bf16[8,128,768]{2,1,0:T(8,128)(2,1)}, bf16[2048,768]{1,0:T(...) custom-call(bf16[2,8,128,768]{3,2,1,0:T(8,128)(2,1)} %bitcast.36, ...), custom_call_target="tpu_custom_call" | custom-call | tf_op jit(solution)/shard_map/front/pallas_call | solution.py:1986
  119.6 87.6 %feed.1 = (bf16[2048,768]{1,0:T(8,128)(2,1)}, bf16[2048,768]{1,0:T(8,128)(2,1)}, bf16[4,768,768]{2,1,0:T(8,128)(2,1)}, bf16[4,768,768]{2,1,0:T(8,128)(2,1)}, f32...) custom-call(bf16[2048,768]{1,0:T(8,128)(2,1)} %bitcast.35, f32[17,768]{1,0:T(8,128)} %vec_ref.9, ...), custom_call_target="tpu_custom_call" | custom-call | tf_op jit(solution)/shard_map/feed/pallas_call | solution.py:677
  207.2 55.2 %back_two.1 = (bf16[16,128,768]{2,1,0:T(8,128)(2,1)}, bf16[2,2,2,384,768]{4,3,2,1,0:T(8,128)(2,1)}, f32[8,768]{1,0:T(8,128)}, bf16[384,768]{1,0:T(8,128)(2,1)}, bf16[384,768]{1,0:T(8,128)(2,1)}) custom-call(bf16[16,128,768]{2,1,0:T(8,128)(2,1)} %get-tuple-element.55.x_ref, bf16[16,128,768]{2,1,0:T(8,128)(2,1)} %bitcast.34, bf16[16,768,768]{2,1,0:T(8,128)(2,1)} %bitcast.22, ...), custom_call_target="tpu_custom_call" | custom-call | tf_op jit(solution)/shard_map/back_two/pallas_call | solution.py:1138
  262.4 58.3 %back_one.1 = (bf16[2,2,384,768]{3,2,1,0:T(8,128)(2,1)}, f32[8,768]{1,0:T(8,128)}, bf16[384,768]{1,0:T(8,128)(2,1)}, bf16[384,768]{1,0:T(8,128)(2,1)}, bf16[2,8,...) custom-call(bf16[2048,768]{1,0:T(8,128)(2,1)} %bitcast.32, ...), custom_call_target="tpu_custom_call", output_to_operand_aliasing={{5}: (14, {})} | custom-call | tf_op jit(solution)/shard_map/back_one/pallas_call | solution.py:1300
  320.7 62.9 %update.1 = (f32[384,768]{1,0:T(8,128)}, bf16[768,768]{1,0:T(8,128)(2,1)}, f32[17,768]{1,0:T(8,128)}, f32[17,768]{1,0:T(8,128)}, bf16[4,128,768]{2,1,0:T(8,128)(2,1)}) custom-call(bf16[2,2,2,192,768]{4,3,2,1,0:T(8,128)(2,1)} %bitcast.37, bf16[4,128,768]{2,1,0:T(8,128)(2,1)} %get-tuple-element.81.late_ref, bf16[384,768]{1,0:T(8,128)(2,1)} %get-tuple-element.82.two_ref, ...), custom_call_target="tpu_custom_call" | custom-call | tf_op jit(solution)/shard_map/update/pallas_call | solution.py:1470
  383.6 10.1 %finish.1 = (f32[384,768]{1,0:T(8,128)}, bf16[384,768]{1,0:T(8,128)(2,1)}, f32[384,768]{1,0:T(8,128)}, f32[17,768]{1,0:T(8,128)}, f32[17,768]{1,0:T(8,128)}, /*i...) custom-call(bf16[768,768]{1,0:T(8,128)(2,1)} %get-tuple-element.87.full, f32[384,768]{1,0:T(8,128)} %bitcast.31, ...), custom_call_target="tpu_custom_call" | custom-call | tf_op jit(solution)/shard_map/finish/pallas_call | solution.py:1557
